TPU v7x, 128 devices: a whole 4x4x4 slice. The times are simulated.
128 devices in a mesh: gx: 4 (over y), gy: 4 (over z), gz: 8 (over x, core).
Axes of the slice: x: 4, y: 4, z: 4, core: 2. Of those that a mesh axis runs over, the one named last changes fastest.
Arguments:
- emission: bfloat16 [3, 256, 1024, 512], P(None, 'gz', 'gx', 'gy'), may hold values from 0 to 2
- absorption: bfloat16 [256, 1024, 512], P('gz', 'gx', 'gy'), may hold values from 0.19921875 to 5
- target_z: bfloat16 [3, 1024, 1024], replicated, may hold values from 0 to 2
- target_x: bfloat16 [3, 256, 1024], replicated, may hold values from 0 to 2
- owner_z: int32 [4, 4, 256, 1], replicated, may hold values from 0 to 31; in each aligned block of 256 rows (0 to 255, 256 to 511, ..., all dimensions but the last counted through in order) at most 16 rows name the same one
- owner_x: int32 [4, 8, 32, 1], replicated, may hold values from 0 to 15; in each aligned block of 32 rows (0 to 31, 32 to 63, ..., all dimensions but the last counted through in order) at most 4 rows name the same one
Outputs:
- grad_emission: bfloat16 [3, 256, 1024, 512], P(None, 'gz', 'gx', 'gy')
- grad_absorption: bfloat16 [256, 1024, 512], P('gz', 'gx', 'gy')
- owned_error: float32 [4, 4, 8], P('gx', 'gy', 'gz')
Inputs may be any that keep to these rules, and one draw needn't show every extreme that they name: Within each block owner_z[a, b, :, 0] of 256 tiles no value appears more than 16 times. Within each block owner_x[b, c, :, 0] of 32 tiles no value appears more than 4 times.
All inputs are finite; a program needn't handle non-finite values.
Results may differ from a plain program's by a relative error of at most 0.001.
Values sent between devices are 32-bit elements; how exact they have to be, the bound alone decides.
A program may use at most 256 MiB of HBM per device.

v0:
```python
import jax
import jax.numpy as jnp
from jax import lax
from jax.sharding import PartitionSpec as P

OPTICAL = 1.5
BACKLIGHT = 1.0
HIGHEST = lax.Precision.HIGHEST


def interp_table(width):
    pixels = jnp.arange(2 * width, dtype=jnp.int32)
    nearest = pixels // 2
    second = jnp.clip(nearest + 2 * (pixels % 2) - 1, 0, width - 1)
    columns = jnp.arange(width, dtype=jnp.int32)
    first_hit = (columns[None, :] == nearest[:, None]).astype(jnp.float32)
    second_hit = (columns[None, :] == second[:, None]).astype(jnp.float32)
    return 0.75 * first_hit + 0.25 * second_hit


def prefix_along(sample_values, axis, upper):
    length = sample_values.shape[axis]
    indices = jnp.arange(length, dtype=jnp.int32)
    if upper:
        chosen = indices[None, :] > indices[:, None]
    else:
        chosen = indices[None, :] < indices[:, None]
    summing = chosen.astype(jnp.float32)
    if axis == 0:
        return jnp.einsum("kj,jab->kab", summing, sample_values, precision=HIGHEST)
    return jnp.einsum("kj,ajb->akb", summing, sample_values, precision=HIGHEST)


def local_forward(emis_up, sigma_up, axis, march_step):
    optical = march_step * sigma_up
    depth_sum = prefix_along(optical, axis, False)
    through = jnp.exp(-depth_sum)
    beyond = jnp.exp(-(depth_sum + optical))
    shares = through - beyond
    colour = jnp.sum(shares[None] * emis_up, axis=axis + 1)
    exit_trans = lax.index_in_dim(beyond, beyond.shape[axis] - 1, axis, keepdims=False)
    return (colour, exit_trans, shares, beyond)


def local_backward(emis_up, shares, beyond, exit_trans, g_colour, g_trans, axis, march_step):
    widened = jnp.expand_dims(g_colour, axis + 1)
    gradient_emission_fine = widened * shares[None]
    inner_sum = jnp.sum(widened * emis_up, axis=0)
    behind = prefix_along(shares * inner_sum, axis, True)
    gradient_optical_depth = (
        beyond * inner_sum - behind - jnp.expand_dims(exit_trans * g_trans, axis)
    )
    return (gradient_emission_fine, march_step * gradient_optical_depth)


def even_merge(arrived, target_rows, march_step):
    layers = arrived.shape[1]
    ahead_trans = jnp.ones(arrived.shape[2:], jnp.float32)
    rendered = jnp.zeros((3,) + arrived.shape[2:], jnp.float32)
    fronts = []
    for position in range(layers):
        portion = arrived[:, position]
        fronts.append(ahead_trans)
        rendered = rendered + ahead_trans[None] * portion[:3]
        ahead_trans = ahead_trans * portion[3]
    rendered = rendered + ahead_trans[None] * BACKLIGHT
    render_residual = rendered - target_rows.astype(jnp.float32)
    g_image = render_residual / march_step
    behind = jnp.full(rendered.shape, BACKLIGHT, jnp.float32)
    replies = [None] * layers
    for position in reversed(range(layers)):
        portion = arrived[:, position]
        g_colour = fronts[position][None] * g_image
        g_trans = fronts[position] * jnp.sum(g_image * behind, axis=0)
        replies[position] = jnp.concatenate([g_colour, g_trans[None]], axis=0)
        behind = portion[:3] + portion[3][None] * behind
    return (jnp.stack(replies, axis=1), jnp.sum(render_residual * render_residual, axis=(0, 2)))


def local(emission, absorption, target_z, target_x, owner_z, owner_x):
    depth_z, width_x, width_y = absorption.shape
    pixels = 2 * width_y
    count_x = lax.axis_size("gx")
    count_y = lax.axis_size("gy")
    count_z = lax.axis_size("gz")
    index_x = lax.axis_index("gx")
    index_y = lax.axis_index("gy")
    index_z = lax.axis_index("gz")
    step_z = OPTICAL / (depth_z * count_z)
    step_x = OPTICAL / (width_x * count_x)
    interp = interp_table(width_y)
    narrow = interp.T.astype(jnp.bfloat16)
    emis_up = jnp.dot(
        emission.reshape(-1, width_y), narrow, preferred_element_type=jnp.float32
    ).reshape(3, depth_z, width_x, pixels)
    sigma_up = jnp.dot(
        absorption.reshape(-1, width_y), narrow, preferred_element_type=jnp.float32
    ).reshape(depth_z, width_x, pixels)
    colour_z, exit_z, shares_z, beyond_z = local_forward(emis_up, sigma_up, 0, step_z)
    colour_x, exit_x, shares_x, beyond_x = local_forward(emis_up, sigma_up, 1, step_x)
    group_z = count_y * count_z
    group_x = count_x * count_y
    slots_z = 2 * width_x // group_z
    slots_x = 2 * depth_z // group_x
    devices = count_x * count_y * count_z
    slab_rows_z = lax.dynamic_index_in_dim(owner_z, index_x, 0, keepdims=False)[..., 0]
    row_z = lax.dynamic_index_in_dim(slab_rows_z, index_y, 0, keepdims=False)
    slab_rows_x = lax.dynamic_index_in_dim(owner_x, index_z, 1, keepdims=False)[..., 0]
    row_x = lax.dynamic_index_in_dim(slab_rows_x, index_y, 0, keepdims=False)
    footprint_z = jnp.concatenate([colour_z, exit_z[None]], axis=0)[:, None]
    footprint_x = jnp.concatenate([colour_x, exit_x[None]], axis=0)[:, None]
    got_z = lax.all_to_all(footprint_z, "gz", split_axis=2, concat_axis=1, tiled=True)
    got_x = lax.all_to_all(footprint_x, "gx", split_axis=2, concat_axis=1, tiled=True)
    share_z = got_z.shape[2]
    share_x = got_x.shape[2]
    window_z = lax.dynamic_slice(
        target_z, (0, index_x * width_x + index_z * share_z, index_y * pixels), (3, share_z, pixels)
    )
    window_x = lax.dynamic_slice(
        target_x, (0, index_z * depth_z + index_x * share_x, index_y * pixels), (3, share_x, pixels)
    )
    reply_z, tile_err_z = even_merge(got_z, window_z, step_z)
    reply_x, tile_err_x = even_merge(got_x, window_x, step_x)
    back_z = lax.all_to_all(reply_z, "gz", split_axis=1, concat_axis=2, tiled=True)[:, 0]
    back_x = lax.all_to_all(reply_x, "gx", split_axis=1, concat_axis=2, tiled=True)[:, 0]
    adj_colour_z, adj_trans_z = (back_z[:3], back_z[3])
    adj_colour_x, adj_trans_x = (back_x[:3], back_x[3])
    labels = jnp.arange(devices, dtype=jnp.int32)
    owner_id_z = index_x * group_z + lax.dynamic_slice_in_dim(row_z, index_z * share_z, share_z, 0)
    owner_id_x = lax.dynamic_slice_in_dim(row_x, index_x * share_x, share_x, 0) * count_z + index_z
    spread = jnp.sum(
        jnp.where(owner_id_z[:, None] == labels[None, :], tile_err_z[:, None], 0.0), axis=0
    )
    spread = spread + jnp.sum(
        jnp.where(owner_id_x[:, None] == labels[None, :], tile_err_x[:, None], 0.0), axis=0
    )
    owned = lax.psum_scatter(spread, ("gx", "gy", "gz"), scatter_dimension=0, tiled=True)
    g_emis_z, g_sigma_z = local_backward(
        emis_up, shares_z, beyond_z, exit_z, adj_colour_z, adj_trans_z, 0, step_z
    )
    g_emis_x, g_sigma_x = local_backward(
        emis_up, shares_x, beyond_x, exit_x, adj_colour_x, adj_trans_x, 1, step_x
    )
    grad_emission = jnp.dot((g_emis_z + g_emis_x).reshape(-1, pixels), interp, precision=HIGHEST)
    grad_emission = grad_emission.reshape(3, depth_z, width_x, width_y).astype(jnp.bfloat16)
    grad_absorption = jnp.dot(
        (g_sigma_z + g_sigma_x).reshape(-1, pixels), interp, precision=HIGHEST
    )
    grad_absorption = grad_absorption.reshape(depth_z, width_x, width_y).astype(jnp.bfloat16)
    owned_error = (owned / (3.0 * pixels * (slots_z + slots_x))).reshape(1, 1, 1)
    return (grad_emission, grad_absorption, owned_error)


def solution(mesh):
    return jax.shard_map(
        local,
        mesh=mesh,
        in_specs=(P(None, "gz", "gx", "gy"), P("gz", "gx", "gy"), P(), P(), P(), P()),
        out_specs=(P(None, "gz", "gx", "gy"), P("gz", "gx", "gy"), P("gx", "gy", "gz")),
        check_vma=False,
    )
```

profile of v0, /device:TPU:1, one launch (start us, length us, event | category | flops | bytes accessed | tf_op | source)
XLA Modules:
  0.0 423.6 jit_solution(10151117695916823625)
XLA Ops:
  0.7 1.6 copy-done
  2.2 4.5 %broadcast_multiply_fusion.1 = (f32[256,8192]{1,0:T(8,128)}, f32[256,8192]{1,0:T(8,128)S(1)}) fusion(bf16[8192,128]{1,0:T(8,128)(2,1)S(1)} %bitcast.414, s32[256]{0:T(256)S(1)} %get-tuple-element.106, s32[256]{0:T(256)S(1)} %get-tuple-element.105), kind=kOutput, calls=%fused_computation.34 | convolution fusion | flops 541261824 | bytes 18876416 | tf_op jit(solution)/shard_map/dot_general | solution.py:96
  6.7 3.5 copy.237
  10.2 3.2 copy-done.5
  13.4 6.4 %fusion.31 = f32[32,256,256]{2,0,1:T(8,128)} fusion(f32[32,256,256]{1,0,2:T(8,128)S(1)} %bitcast.417), kind=kOutput, calls=%fused_computation.42 | convolution fusion | flops 6442516480 | bytes 16777216 | tf_op jit(solution)/shard_map/kj,ajb->akb/dot_general | solution.py:31
  19.8 10.5 %copy.182 = f32[32,256,256]{2,0,1:T(8,128)} copy(f32[32,256,256]{1,0,2:T(8,128)} %bitcast.418) | data formatting | bytes 16777216 | tf_op jit(solution)/shard_map/mul | solution.py:35
  30.3 10.5 %copy.181 = f32[32,256,256]{1,0,2:T(8,128)} copy(f32[32,256,256]{2,0,1:T(8,128)} %fusion.31) | data formatting | bytes 16777216 | tf_op jit(solution)/shard_map/kj,ajb->akb/dot_general | solution.py:31
  40.8 9.3 %fusion.12 = (f32[32,256,256]{2,0,1:T(8,128)}, f32[32,256,256]{2,0,1:T(8,128)S(1)}) fusion(f32[32,256,256]{1,0,2:T(8,128)} %copy.181, f32[32,256,256]{2,0,1:T(8,128)} %copy.182), kind=kLoop, calls=%fused_computation.20 | loop fusion | flops 8388608 | bytes 33554432 | tf_op jit(solution)/shard_map/sub | solution.py:39
  50.1 3.2 copy-done.6
  53.3 12.8 %convolution_bitcast_fusion = f32[24576,256]{0,1:T(8,128)} fusion(bf16[24576,128]{1,0:T(8,128)(2,1)} %bitcast.424, s32[256]{0:T(256)S(1)} %get-tuple-element.106, s32[256]{0:T(256)S(1)} %get-tuple-element.105), kind=kOutput, calls=%fused_computation | convolution fusion | flops 1610809344 | bytes 31459328 | tf_op jit(solution)/shard_map/dot_general | solution.py:93
  66.1 24.7 %copy.208 = f32[24576,256]{1,0:T(8,128)} copy(f32[24576,256]{0,1:T(8,128)} %convolution_bitcast_fusion) | data formatting | bytes 50331648 | tf_op jit(solution)/shard_map/reshape | solution.py:95
  90.8 10.0 %copy.236 = f32[32,8,32,256]{3,2,1,0:T(8,128)} copy(f32[32,8,32,256]{3,1,2,0:T(8,128)} %bitcast.419) | data formatting | bytes 16777216
  100.8 10.9 %copy.157 = f32[32,256,256]{2,0,1:T(8,128)} copy(f32[32,256,256]{1,0,2:T(8,128)} %bitcast.421) | data formatting | bytes 16777216 | tf_op jit(solution)/shard_map/mul | solution.py:35
  111.7 15.7 %exponential_subtract_fusion = (f32[32,256,256]{2,0,1:T(8,128)S(1)}, f32[32,256,256]{2,0,1:T(8,128)}) fusion(f32[32,256,256]{2,0,1:T(8,128)} %copy.157), kind=kOutput, calls=%fused_computation.30 | convolution fusion | flops 813696000 | bytes 25165824 | tf_op jit(solution)/shard_map/kj,jab->kab/dot_general | solution.py:30
  127.3 4.9 %copy.159 = f32[32,256,256]{2,1,0:T(8,128)S(1)} copy(f32[32,256,256]{2,0,1:T(8,128)S(1)} %get-tuple-element.50) | data formatting | bytes 16777216 | tf_op jit(solution)/shard_map/sub | solution.py:39
  132.2 11.4 %copy.183 = f32[32,256,256]{2,1,0:T(8,128)S(1)} copy(f32[32,256,256]{2,0,1:T(8,128)} %get-tuple-element.48) | data formatting | bytes 16777216 | tf_op jit(solution)/shard_map/sub | solution.py:39
  143.7 14.2 %multiply_reduce_fusion.3 = (f32[3,256,256]{2,1,0:T(8,128)S(1)}, f32[3,32,256]{2,1,0:T(8,128)S(1)}) fusion(f32[3,32,256,256]{3,2,1,0:T(8,128)} %bitcast.415, f32[32,256,256]{2,1,0:T(8,128)S(1)} %copy.159, f32[32,256,256]{2,1,0:T(8,128)S(1)} %copy.183), kind=kLoop, calls=%fused_computation.8 | loop fusion | flops 24944640 | bytes 42827776 | tf_op jit(solution)/shard_map/reduce_sum | solution.py:40
  157.9 0.7 copy.185
  158.7 5.0 %all-to-all-start.2 = ((f32[4,1,32,256]{3,0,1,2:T(4,128)}), f32[4,1,32,256]{3,0,1,2:T(4,128)S(1)}, u32[]{:S(2)}, u32[]{:S(2)}) async-start(f32[4,1,32,256]{3,0,1,2:T(4,128)} %copy.185), calls=%async_computation.2 | async-start | bytes 262144 | tf_op jit(solution)/shard_map/all_to_all | solution.py:113
  163.7 1.8 slice.252
  165.6 1.6 copy.162
  167.3 1.2 all-to-all-done.2
  168.5 6.4 %all-to-all-start = ((f32[4,1,256,256]{3,0,1,2:T(4,128)}), f32[4,1,256,256]{3,0,1,2:T(4,128)S(1)}, u32[]{:S(2)}, u32[]{:S(2)}) async-start(f32[4,1,256,256]{3,0,1,2:T(4,128)} %copy.162), calls=%async_computation | async-start | bytes 2097152 | tf_op jit(solution)/shard_map/all_to_all | solution.py:112
  175.1 0.7 broadcast_multiply_fusion.20
  176.0 0.7 pad_maximum_fusion
  176.7 13.3 %all-to-all-done = f32[4,1,256,256]{3,0,1,2:T(4,128)S(1)} async-done(((f32[4,1,256,256]{3,0,1,2:T(4,128)}), f32[4,1,256,256]{3,0,1,2:T(4,128)S(1)}, u32[]{:S(2)}, u32[]{:S(2)}) %all-to-all-start) | async-done | bytes 1048608 | tf_op jit(solution)/shard_map/all_to_all | solution.py:112
  190.0 3.3 all-to-all-start.3
  194.2 1.0 broadcast_multiply_fusion.2
  195.4 0.7 fusion.35
  196.1 0.7 fusion.36
  196.8 0.7 fusion.37
  197.4 0.7 fusion.38
  198.1 0.7 fusion.39
  198.8 0.7 fusion.40
  199.5 0.7 fusion.41
  200.8 4.3 %all-to-all-start.1 = ((f32[4,8,32,256]{3,2,0,1:T(8,128)}), f32[4,8,32,256]{3,2,0,1:T(8,128)S(1)}, u32[]{:S(2)}, u32[]{:S(2)}) async-start(f32[4,8,32,256]{3,2,0,1:T(8,128)} %fusion.42), calls=%async_computation.1 | async-start | bytes 2097152 | tf_op jit(solution)/shard_map/all_to_all | solution.py:124
  205.1 0.7 fusion.87
  205.9 0.8 fusion.84
  206.7 0.8 fusion.66
  207.6 70.9 %all-reduce = f32[128]{0:T(128)S(1)} all-reduce(f32[128]{0:T(128)S(1)} %add.273), channel_id=2, replica_groups=mesh['gx'=4,'gy'=4,'gz'=8] {'gx','gy','gz'}, use_global_device_ids=true, to_apply=%region_20.21.clone | all-reduce | flops 128 | bytes 1024
  279.8 24.5 %fusion.24 = bf16[3,32,256,128]{3,2,1,0:T(8,128)(2,1)} fusion(f32[3,32,256]{2,1,0:T(8,128)S(1)} %copy_bitcast_fusion.1, f32[32,256,256]{2,1,0:T(8,128)} %copy-done.3, f32[3,256,256]{2,1,0:T(8,128)S(1)} %bitcast.422, f32[32,256,256]{2,1,0:T(8,128)} %copy-done.2, s32[256]{0:T(256)S(1)} %get-tuple-element.106, s32[256]{0:T(256)S(1)} %get-tuple-element.105), kind=kOutput, calls=%fused_computation.35 | convolution fusion | flops 9685860352 | bytes 23955456 | tf_op jit(solution)/shard_map/dot_general | solution.py:144
  304.3 21.2 %multiply_reduce_fusion.1 = (f32[32,256,256]{2,1,0:T(8,128)}, f32[32,256,256]{2,1,0:T(8,128)}) fusion(f32[3,32,256,256]{3,2,1,0:T(8,128)} %bitcast.416, f32[3,256,256]{2,1,0:T(8,128)S(1)} %bitcast.423, f32[3,32,256]{2,1,0:T(8,128)S(1)} %copy_bitcast_fusion.1), kind=kLoop, calls=%fused_computation.2 | loop fusion | flops 20971520 | bytes 42827776 | tf_op jit(solution)/shard_map/reduce_sum | solution.py:48
  325.5 14.1 %copy_multiply_fusion = f32[32,256,256]{2,0,1:T(8,128)} fusion(f32[32,256,256]{2,0,1:T(8,128)} %get-tuple-element.48, f32[32,256,256]{2,1,0:T(8,128)} %get-tuple-element.4), kind=kLoop, calls=%fused_computation.31 | loop fusion | flops 2097152 | bytes 25165824 | tf_op jit(solution)/shard_map/mul | solution.py:49
  339.6 16.9 %fusion.17 = f32[32,256,256]{2,1,0:T(8,128)} fusion(f32[32,256,256]{2,0,1:T(8,128)} %copy_multiply_fusion), kind=kOutput, calls=%fused_computation.25 | convolution fusion | flops 6442516480 | bytes 16777216 | tf_op jit(solution)/shard_map/kj,ajb->akb/dot_general | solution.py:31
  356.5 10.3 %copy.202 = f32[32,256,256]{1,0,2:T(8,128)} copy(f32[32,256,256]{2,1,0:T(8,128)} %fusion.17) | data formatting | bytes 16777216 | tf_op jit(solution)/shard_map/kj,ajb->akb/dot_general | solution.py:31
  367.1 1.9 slice_multiply_fusion
  369.0 38.1 %fusion.10 = f32[32,256,256]{2,0,1:T(8,128)} fusion(f32[32,256,256]{1,0,2:T(8,128)} %copy.202, f32[32,256,256]{2,0,1:T(8,128)} %copy-done.6, f32[32,256,256]{2,0,1:T(8,128)} %get-tuple-element.51, f32[32,256,256]{2,1,0:T(8,128)} %get-tuple-element.4, f32[32,256,256]{2,1,0:T(8,128)} %get-tuple-element.3, f32[32,256,256]{2,0,1:T(8,128)} %copy-done.4, ...), kind=kOutput, calls=%fused_computation.16 | convolution fusion | flops 826278912 | bytes 59015168 | tf_op jit(solution)/shard_map/kj,jab->kab/dot_general | solution.py:30
  407.1 15.1 %fusion.27 = bf16[32,256,128]{2,1,0:T(8,128)(2,1)} fusion(f32[32,256,256]{2,0,1:T(8,128)} %fusion.10, s32[256]{0:T(256)S(1)} %get-tuple-element.106, s32[256]{0:T(256)S(1)} %get-tuple-element.105), kind=kOutput, calls=%fused_computation.36 | convolution fusion | flops 3222437888 | bytes 10487808 | tf_op jit(solution)/shard_map/dot_general | solution.py:146
  (65 shorter events, 3.2 us)
Async XLA Ops:
  0.6 1.6 copy-start
  10.2 3.2 copy-start.5
  50.1 3.2 copy-start.6
  127.3 4.9 %copy-start.4 = (f32[32,256,256]{2,0,1:T(8,128)}, f32[32,256,256]{2,0,1:T(8,128)S(1)}, u32[]{:S(2)}) copy-start(f32[32,256,256]{2,0,1:T(8,128)S(1)} %get-tuple-element.50) | copy-start | bytes 25165828
  132.2 11.5 %copy-start.2 = (f32[32,256,256]{2,1,0:T(8,128)}, f32[32,256,256]{2,1,0:T(8,128)S(1)}, u32[]{:S(2)}) copy-start(f32[32,256,256]{2,1,0:T(8,128)S(1)} %copy.159) | copy-start | bytes 25165828
  143.6 14.3 %copy-start.3 = (f32[32,256,256]{2,1,0:T(8,128)}, f32[32,256,256]{2,1,0:T(8,128)S(1)}, u32[]{:S(2)}) copy-start(f32[32,256,256]{2,1,0:T(8,128)S(1)} %copy.183) | copy-start | bytes 25165828
  158.7 9.8 %all-to-all-start.2 = ((f32[4,1,32,256]{3,0,1,2:T(4,128)}), f32[4,1,32,256]{3,0,1,2:T(4,128)S(1)}, u32[]{:S(2)}, u32[]{:S(2)}) async-start(f32[4,1,32,256]{3,0,1,2:T(4,128)} %copy.185), calls=%async_computation.2 | async-start | bytes 262144 | tf_op jit(solution)/shard_map/all_to_all | solution.py:113
  168.5 21.5 %all-to-all-start = ((f32[4,1,256,256]{3,0,1,2:T(4,128)}), f32[4,1,256,256]{3,0,1,2:T(4,128)S(1)}, u32[]{:S(2)}, u32[]{:S(2)}) async-start(f32[4,1,256,256]{3,0,1,2:T(4,128)} %copy.162), calls=%async_computation | async-start | bytes 2097152 | tf_op jit(solution)/shard_map/all_to_all | solution.py:112
  190.0 10.8 %all-to-all-start.3 = ((f32[4,4,8,256]{3,2,0,1:T(8,128)}), f32[4,4,8,256]{3,2,0,1:T(8,128)S(1)}, u32[]{:S(2)}, u32[]{:S(2)}) async-start(f32[4,4,8,256]{3,2,0,1:T(8,128)} %pad_maximum_fusion), calls=%async_computation.3 | async-start | bytes 262144 | tf_op jit(solution)/shard_map/all_to_all | solution.py:125
  200.8 78.9 %all-to-all-start.1 = ((f32[4,8,32,256]{3,2,0,1:T(8,128)}), f32[4,8,32,256]{3,2,0,1:T(8,128)S(1)}, u32[]{:S(2)}, u32[]{:S(2)}) async-start(f32[4,8,32,256]{3,2,0,1:T(8,128)} %fusion.42), calls=%async_computation.1 | async-start | bytes 2097152 | tf_op jit(solution)/shard_map/all_to_all | solution.py:124
  369.0 53.2 %copy-start.1 = (bf16[32,256,128]{2,1,0:T(8,128)(2,1)S(1)}, bf16[32,256,128]{2,1,0:T(8,128)(2,1)}, u32[]{:S(2)}) copy-start(bf16[32,256,128]{2,1,0:T(8,128)(2,1)} %param.7) | copy-start | bytes 6291460
where the time goes:
time: 430 us; the launch traced here: 424 us
  matrix products  134 us (31%)
  local copies, waits for them, and re-layouts  110 us (26%)
  other arithmetic  71.6 us (17%)
  blocking collectives  70.9 us (16%)
  starting transfers between devices  19.1 us (4%)
  waiting for transfers between devices  14.6 us (3%)
    unnamed x1, blocking collectives  70.9 us
    dot_general x2, matrix products, prefix_along(): return jnp.einsum('kj,jab->kab', summing, sample_values, precision=HIGHEST)  53.7 us
    reshape x1, local copies, waits for them, and re-layouts, local(): emis_up = jnp.dot(emission.reshape(-1, width_y), narrow, preferred_elemen...  24.7 us
    dot_general x1, matrix products, local(): jnp.dot((g_emis_z + g_emis_x).reshape(-1, pixels), interp, precision=HIGH...  24.5 us
    dot_general x2, matrix products, prefix_along(): return jnp.einsum('kj,ajb->akb', summing, sample_values, precision=HIGHEST)  23.3 us
    unnamed x31, local copies, waits for them, and re-layouts  22.2 us
    mul x2, local copies, waits for them, and re-layouts, local_forward(): optical = march_step * sigma_up  21.4 us
    reduce_sum x1, other arithmetic, local_backward(): inner_sum = jnp.sum(widened * emis_up, axis=0)  21.2 us
  transfers between devices with their start and end apart: 4, of which 2 were waited for; matrix products, arithmetic and copies ran while one was open for 4% of the time, Pallas kernels for 0%

commit v1 on v0

v1 whole, which is shorter than its diff:
```python
import functools
import math

import jax
import jax.numpy as jnp
import numpy as np
from jax import lax
from jax.experimental import pallas as pl
from jax.experimental.pallas import tpu as pltpu
from jax.sharding import PartitionSpec as P

F32 = jnp.float32
BF16 = jnp.bfloat16
OPTICAL = 1.5
BACKLIGHT = 1.0

NSEG = 8
SEG = 32
HALF = 16
PITCH = 20
ZG = 4
NZ = 32
NZG = NZ // ZG
STEPS = 2 * NZG
XU = 4
LANE = 128


def interp_table(width):
    pixels = np.arange(2 * width)
    nearest = pixels // 2
    second = np.clip(nearest + 2 * (pixels % 2) - 1, 0, width - 1)
    columns = np.arange(width)
    return 0.75 * (columns[None, :] == nearest[:, None]) + 0.25 * (columns[None, :] == second[:, None])


def half(h):
    return slice(h * LANE, (h + 1) * LANE)


def upsample_store(fine, f, z, r):
    for s in range(NSEG):
        for h in range(2):
            fine[f, z, h, s * PITCH : s * PITCH + HALF] = r[s * HALF : (s + 1) * HALF, half(h)]


def upsample_part(ebuf, sbuf, tab, fine, h, z):
    rows = NSEG * HALF
    if h == 0:
        a = jnp.concatenate([ebuf[0, z].reshape(rows, LANE), ebuf[1, z].reshape(rows, LANE)], axis=0)
        r = jnp.dot(a, tab[0:LANE], preferred_element_type=F32)
        upsample_store(fine, 0, z, r[:rows])
        upsample_store(fine, 1, z, r[rows:])
    else:
        r = jnp.dot(ebuf[2, z].reshape(rows, LANE), tab[0:LANE], preferred_element_type=F32)
        upsample_store(fine, 2, z, r)
        s = sbuf[z].reshape(rows, LANE)
        r = jnp.dot(jnp.concatenate([s, s], axis=1), tab[LANE:], preferred_element_type=F32)
        upsample_store(fine, 3, z, r)


class Loader:
    def __init__(self, e_hbm, s_hbm, ebufs, sbufs, sems):
        self.refs = (e_hbm, s_hbm, ebufs, sbufs, sems)

    def copies(self, t, b):
        e_hbm, s_hbm, ebufs, sbufs, sems = self.refs
        k, zg = t // NZG, t % NZG
        zs, xs = pl.ds(zg * ZG, ZG), pl.ds(pl.multiple_of(k * HALF, HALF), HALF)
        return (
            pltpu.make_async_copy(e_hbm.at[:, zs, :, xs, :], ebufs[b], sems.at[b, 0]),
            pltpu.make_async_copy(s_hbm.at[zs, :, xs, :], sbufs[b], sems.at[b, 1]),
        )

    def start(self, t, b):
        for c in self.copies(t, b):
            c.start()

    def wait(self, t, b):
        for c in self.copies(t, b):
            c.wait()


def forward_scan(fine, zs, zc, xc, k, zg, extra):
    for h in range(2):
        hs = half(h)
        rows = [pl.ds(pl.multiple_of((zg * ZG + z) * NSEG, NSEG), NSEG) for z in range(ZG)]
        start = tuple(xc[i, h, rows[z], :] for z in range(ZG) for i in range(5))

        def step(j, carry):
            carry = list(carry)
            extra(h, j)
            for u in range(XU):
                xm = j * XU + u
                zr = k * HALF + xm
                s_z = zs[zr, :, hs]
                c0, c1, c2, t_z = [zc[zr, i, :, hs] for i in range(4)]
                for z in range(ZG):
                    e0, e1, e2, sg = [fine[f, z, h, pl.ds(xm, NSEG, stride=PITCH), :] for f in range(4)]
                    s_z = s_z + sg
                    t_new = jnp.exp2(s_z)
                    share = t_z - t_new
                    t_z = t_new
                    c0 = c0 + share * e0
                    c1 = c1 + share * e1
                    c2 = c2 + share * e2
                    s_x, t_x, d0, d1, d2 = carry[z * 5 : z * 5 + 5]
                    s_x = s_x + sg
                    t_new = jnp.exp2(s_x * 0.25)
                    share = t_x - t_new
                    carry[z * 5 : z * 5 + 5] = [s_x, t_new, d0 + share * e0, d1 + share * e1, d2 + share * e2]
                zs[zr, :, hs] = s_z
                for i, v in enumerate((c0, c1, c2, t_z)):
                    zc[zr, i, :, hs] = v
            return tuple(carry)

        carry = lax.fori_loop(0, HALF // XU, step, start)
        for z in range(ZG):
            for i in range(5):
                xc[i, h, rows[z], :] = carry[z * 5 + i]


def compose(front, back):
    c0, c1, c2, t = front
    d0, d1, d2, u = back
    return (c0 + t * d0, c1 + t * d1, c2 + t * d2, t * u)


def merge(bricks, target, inv_step):
    ahead = (jnp.zeros_like(target[0]),) * 3 + (jnp.ones_like(target[0]),)
    fronts = []
    for brick in bricks:
        fronts.append(ahead[3])
        ahead = compose(ahead, brick)
    resid = [ahead[c] + ahead[3] * BACKLIGHT - target[c] for c in range(3)]
    g = [r * inv_step for r in resid]
    behind = [jnp.full_like(target[0], BACKLIGHT)] * 3
    replies = []
    for front, brick in reversed(list(zip(fronts, bricks))):
        dot = g[0] * behind[0] + g[1] * behind[1] + g[2] * behind[2]
        replies.append([front * g[0], front * g[1], front * g[2], front * dot])
        behind = [brick[c] + brick[3] * behind[c] for c in range(3)]
    replies.reverse()
    return replies, resid[0] * resid[0] + resid[1] * resid[1] + resid[2] * resid[2]


def forward_kernel(
    inv_z, inv_x,
    e_hbm, s_hbm, tz_hbm, tx_hbm, tab,
    coz, cox, err,
    ebuf0, ebuf1, sbuf0, sbuf1, fine0, fine1, zs, zc, xc,
    tzb, txb, tzf, txf,
    sib, pc, got, rep, back, fin, finr,
    xloc, xgot, xrep, xback, xsuf,
    in_sem, t_sem, sem_sib, sem_chip, sem_rep, sem_fin, sem_x, sem_xr,
):
    ix, iy, iz = lax.axis_index("gx"), lax.axis_index("gy"), lax.axis_index("gz")
    chip, core = iz // 2, iz % 2
    load = Loader(e_hbm, s_hbm, (ebuf0, ebuf1), (sbuf0, sbuf1), in_sem)
    load.start(0, 0)
    load.start(1, 1)
    px = pl.ds(pl.multiple_of(iy * 256, 256), 256)
    tz_copy = pltpu.make_async_copy(tz_hbm.at[:, pl.ds(pl.multiple_of(ix * 256, 256), 256), px], tzb, t_sem.at[0])
    tx_copy = pltpu.make_async_copy(tx_hbm.at[:, pl.ds(pl.multiple_of(iz * NZ, NZ), NZ), px], txb, t_sem.at[1])
    tz_copy.start()
    tx_copy.start()

    sibling = {"gz": chip * 2 + 1 - core}
    chips = [{"gz": lax.rem(chip + d, 4) * 2 + core} for d in (1, 2, 3)]
    slabs = [{"gx": lax.rem(ix + d, 4)} for d in (1, 2, 3)]
    barrier = pltpu.get_barrier_semaphore()
    for peer in [sibling] + chips + slabs:
        pl.semaphore_signal(barrier, inc=1, device_id=peer, device_id_type=pl.DeviceIdType.MESH)

    def remote(src, dst, sems, peer):
        return pltpu.make_async_remote_copy(
            src_ref=src, dst_ref=dst, send_sem=sems.at[0], recv_sem=sems.at[1],
            device_id=peer, device_id_type=pl.DeviceIdType.MESH,
        )

    def sib_copy(k):
        return remote(zc.at[pl.ds(k * HALF + (1 - core) * 8, 8)], sib.at[k], sem_sib.at[k], sibling)

    def chip_copies(k):
        return [
            remote(pc.at[k, pl.ds(lax.rem(chip + d, 4) * 2, 2)], got.at[k, chip], sem_chip.at[k, d - 1], chips[d - 1])
            for d in (1, 2, 3)
        ]

    def rep_copies(k):
        return [
            remote(rep.at[k, lax.rem(chip + d, 4)], back.at[k, pl.ds(chip * 2, 2)], sem_rep.at[k, d - 1], chips[d - 1])
            for d in (1, 2, 3)
        ]

    def fin_copy(k):
        return remote(fin.at[k], finr.at[k], sem_fin.at[k], sibling)

    def x_copies():
        return [remote(xloc.at[lax.rem(ix + d, 4)], xgot.at[ix], sem_x.at[d - 1], slabs[d - 1]) for d in (1, 2, 3)]

    def xr_copies():
        return [remote(xrep.at[lax.rem(ix + d, 4)], xback.at[ix], sem_xr.at[d - 1], slabs[d - 1]) for d in (1, 2, 3)]

    def pair(k, m, hs):
        mine = [zc[k * HALF + core * 8 + m, i, :, hs] for i in range(4)]
        other = [sib[k, m, i, :, hs] for i in range(4)]
        first = core == 0
        return [jnp.where(first, a, b) for a, b in zip(mine, other)], [jnp.where(first, b, a) for a, b in zip(mine, other)]

    def z_compose(k):
        sib_copy(k).wait_recv()

        def body(m, _):
            for h in range(2):
                front, rear = pair(k, m, half(h))
                for i, v in enumerate(compose(front, rear)):
                    pc[k, m, i, :, half(h)] = v
            return 0

        lax.fori_loop(0, 8, body, 0)
        for c in chip_copies(k):
            c.start()

    def z_merge(k):
        for c in chip_copies(k):
            c.wait_recv()
        for i in range(2):
            m = chip * 2 + i
            got[k, chip, i] = pc[k, m]
            sq = jnp.zeros((8, LANE), F32)
            for h in range(2):
                bricks = [[got[k, o, i, f, :, half(h)] for f in range(4)] for o in range(4)]
                row = k * HALF + core * 8 + m
                target = [tzf[c, h, pl.ds(row, NSEG, stride=SEG + 4), :] for c in range(3)]
                replies, s = merge(bricks, target, inv_z)
                sq = sq + s
                for o in range(4):
                    for f in range(4):
                        rep[k, o, i, f, :, half(h)] = replies[o][f]
            err[k * 2 + i] = sq
        for c in rep_copies(k):
            c.start()
        back[k, pl.ds(chip * 2, 2)] = rep[k, chip]

    def z_split(k):
        for c in rep_copies(k):
            c.wait_recv()

        def body(m, _):
            for h in range(2):
                hs = half(h)
                a, b = pair(k, m, hs)
                g0, g1, g2, gt = [back[k, m, f, :, hs] for f in range(4)]
                inner_b = g0 * b[0] + g1 * b[1] + g2 * b[2] + gt * b[3]
                k_b = -(a[3] * inner_b)
                k_a = k_b - (g0 * a[0] + g1 * a[1] + g2 * a[2])
                part_a = (g0, g1, g2, k_a)
                part_b = (a[3] * g0, a[3] * g1, a[3] * g2, k_b)
                first = core == 0
                for f in range(4):
                    coz[k * HALF + core * 8 + m, f, :, hs] = jnp.where(first, part_a[f], part_b[f])
                    fin[k, m, f, :, hs] = jnp.where(first, part_b[f], part_a[f])
            return 0

        lax.fori_loop(0, 8, body, 0)
        fin_copy(k).start()

    def z_finish(k):
        fin_copy(k).wait_recv()
        coz[pl.ds(k * HALF + (1 - core) * 8, 8)] = finr[k]

    def x_compose():
        for g in range(4):
            for h in range(2):
                acc = None
                for s in range(NSEG):
                    rows = pl.ds(g * 64 + s, 8, stride=NSEG)
                    seg = tuple(xc[i, h, rows, :] for i in (2, 3, 4, 1))
                    acc = seg if acc is None else compose(acc, seg)
                for f in range(4):
                    xloc[g, f, :, half(h)] = acc[f]
        for c in x_copies():
            c.start()

    def x_merge():
        for c in x_copies():
            c.wait_recv()
        xgot[ix] = xloc[ix]
        sq = jnp.zeros((8, LANE), F32)
        for h in range(2):
            bricks = [[xgot[o, f, :, half(h)] for f in range(4)] for o in range(4)]
            target = [txf[c, pl.ds(pl.multiple_of(ix * 8, 8), 8), half(h)] for c in range(3)]
            replies, s = merge(bricks, target, inv_x)
            sq = sq + s
            for o in range(4):
                for f in range(4):
                    xrep[o, f, :, half(h)] = replies[o][f]
        err[4] = sq
        for c in xr_copies():
            c.start()
        xback[ix] = xrep[ix]

    def x_split():
        for c in xr_copies():
            c.wait_recv()
        for g in range(4):
            for h in range(2):
                g0, g1, g2, gt = [xback[g, f, :, half(h)] for f in range(4)]
                suffix = None
                for s in reversed(range(NSEG)):
                    rows = pl.ds(g * 64 + s, 8, stride=NSEG)
                    seg = tuple(xc[i, h, rows, :] for i in (2, 3, 4, 1))
                    suffix = seg if suffix is None else compose(seg, suffix)
                    xsuf[s] = g0 * suffix[0] + g1 * suffix[1] + g2 * suffix[2] + gt * suffix[3]
                front = jnp.ones((8, LANE), F32)
                for s in range(NSEG):
                    rows = pl.ds(g * 64 + s, 8, stride=NSEG)
                    cox[0, h, rows, :] = front * g0
                    cox[1, h, rows, :] = front * g1
                    cox[2, h, rows, :] = front * g2
                    cox[3, h, rows, :] = -(front * xsuf[s])
                    front = front * xc[1, h, rows, :]

    zs[...] = jnp.zeros_like(zs)
    xc[0] = jnp.zeros_like(xc[0])
    xc[1] = jnp.ones_like(xc[1])
    for i in (2, 3, 4):
        xc[i] = jnp.zeros_like(xc[i])

    def clear(m, _):
        for f in range(4):
            zc[m, f] = jnp.full((8, 256), float(f == 3), F32)
        return 0

    lax.fori_loop(0, SEG, clear, 0)
    load.wait(0, 0)

    def first(z, _):
        for h in range(2):
            upsample_part(ebuf0, sbuf0, tab, fine0, h, z)
        return 0

    lax.fori_loop(0, ZG, first, 0)

    bufs = ((ebuf0, sbuf0, fine0), (ebuf1, sbuf1, fine1))

    def pair_of_steps(i, _):
        for b in range(2):
            t = i * 2 + b
            k, zg = t // NZG, t % NZG
            other = bufs[1 - b]

            @pl.when(t + 2 < STEPS)
            def _():
                load.start(t + 2, b)

            @pl.when(t + 1 < STEPS)
            def _():
                load.wait(t + 1, 1 - b)

            forward_scan(
                bufs[b][2], zs, zc, xc, k, zg,
                lambda h, z: upsample_part(other[0], other[1], tab, other[2], h, z),
            )

        @pl.when(i == 3)
        def _():
            pl.semaphore_wait(barrier, 7)
            sib_copy(0).start()

        @pl.when(i == 5)
        def _():
            z_compose(0)

        return 0

    lax.fori_loop(0, STEPS // 2, pair_of_steps, 0)
    sib_copy(1).start()
    x_compose()
    tz_copy.wait()
    tx_copy.wait()

    def widen(c, _):
        for h in range(2):
            for s in range(NSEG):
                tzf[c, h, pl.ds(s * (SEG + 4), SEG), :] = tzb[c, pl.ds(s * SEG, SEG), half(h)].astype(F32)
        txf[c] = txb[c].astype(F32)
        return 0

    lax.fori_loop(0, 3, widen, 0)
    z_merge(0)
    z_compose(1)
    x_merge()
    z_split(0)
    x_split()
    z_merge(1)
    z_finish(0)
    z_split(1)
    z_finish(1)
    for k in range(2):
        for c in [sib_copy(k)] + chip_copies(k) + rep_copies(k) + [fin_copy(k)]:
            c.wait_send()
    for c in x_copies() + xr_copies():
        c.wait_send()


def backward_scan(fine, zcar, xcar, coz, cox, hl, k, zg, extra):
    for h in range(2):
        hs = half(h)
        rows = [pl.ds(pl.multiple_of((zg * ZG + z) * NSEG, NSEG), NSEG) for z in range(ZG)]
        start = tuple(xcar[i, h, rows[z], :] for z in range(ZG) for i in range(3))
        gx = [[cox[c, h, rows[z], :] for c in range(3)] for z in range(ZG)]

        def step(j, carry):
            carry = list(carry)
            extra(h, j)
            held = [[[None] * XU for _ in range(4)] for _ in range(ZG)]
            for u in range(XU):
                xm = j * XU + u
                zr = k * HALF + xm
                s_z, t_z, a_z = [zcar[i, zr, :, hs] for i in range(3)]
                g0, g1, g2 = [coz[zr, c, :, hs] for c in range(3)]
                for z in range(ZG):
                    e0, e1, e2, sg = [fine[f, z, h, pl.ds(xm, NSEG, stride=PITCH), :] for f in range(4)]
                    s_z = s_z + sg
                    t_new = jnp.exp2(s_z)
                    share_z = t_z - t_new
                    t_z = t_new
                    inner = g0 * e0 + g1 * e1 + g2 * e2
                    a_z = a_z + share_z * inner
                    grad = t_new * inner + a_z
                    h0, h1, h2 = gx[z]
                    s_x, t_x, a_x = carry[z * 3 : z * 3 + 3]
                    s_x = s_x + sg
                    t_new = jnp.exp2(s_x * 0.25)
                    share_x = t_x - t_new
                    inner = h0 * e0 + h1 * e1 + h2 * e2
                    a_x = a_x + share_x * inner
                    grad = grad + 0.25 * (t_new * inner + a_x)
                    carry[z * 3 : z * 3 + 3] = [s_x, t_new, a_x]
                    held[z][0][u] = g0 * share_z + h0 * share_x
                    held[z][1][u] = g1 * share_z + h1 * share_x
                    held[z][2][u] = g2 * share_z + h2 * share_x
                    held[z][3][u] = grad
                for i, v in enumerate((s_z, t_z, a_z)):
                    zcar[i, zr, :, hs] = v
                if u % 2:
                    for z in range(ZG):
                        for f in range(4):
                            v = jnp.concatenate(held[z][f][u - 1 : u + 1], axis=0)
                            hi = v.astype(BF16)
                            lo = (v - hi.astype(F32)).astype(BF16)
                            r = slice((u - 1) * 8, (u + 1) * 8)
                            hl[f, z, j, r, h * LANE : (h + 1) * LANE] = hi
                            hl[f, z, j, r, (h + 2) * LANE : (h + 3) * LANE] = lo
            return tuple(carry)

        carry = lax.fori_loop(0, HALF // XU, step, start)
        for z in range(ZG):
            for i in range(3):
                xcar[i, h, rows[z], :] = carry[z * 3 + i]


def down_part(hl, down, coarse, eout, sout, h, z):
    rows = NSEG * HALF
    for f in ((0, 1) if h == 0 else (2, 3)):
        a = hl[f, z].reshape(rows, 4 * LANE)
        r = jnp.dot(a, down[int(f == 3)], preferred_element_type=F32)
        for m in range(HALF):
            coarse[f, pl.ds(m, NSEG, stride=PITCH), :] = r[m * 8 : (m + 1) * 8]
        for s in range(NSEG):
            v = coarse[f, pl.ds(s * PITCH, HALF), :].astype(BF16)
            if f == 3:
                sout[z, s] = v
            else:
                eout[f, z, s] = v


def backward_kernel(
    e_hbm, s_hbm, tab, down, coz, cox,
    ge_hbm, gs_hbm,
    ebuf0, ebuf1, sbuf0, sbuf1, fine0, fine1, hl0, hl1, coarse,
    eout0, eout1, sout0, sout1, zcar, xcar,
    in_sem, out_sem,
):
    load = Loader(e_hbm, s_hbm, (ebuf0, ebuf1), (sbuf0, sbuf1), in_sem)
    load.start(0, 0)
    load.start(1, 1)
    eouts, souts = (eout0, eout1), (sout0, sout1)

    def stores(t, b):
        k, zg = t // NZG, t % NZG
        zr, xr = pl.ds(zg * ZG, ZG), pl.ds(pl.multiple_of(k * HALF, HALF), HALF)
        return (
            pltpu.make_async_copy(eouts[b], ge_hbm.at[:, zr, :, xr, :], out_sem.at[b, 0]),
            pltpu.make_async_copy(souts[b], gs_hbm.at[zr, :, xr, :], out_sem.at[b, 1]),
        )

    zcar[0] = jnp.zeros_like(zcar[0])
    zcar[1] = jnp.ones_like(zcar[1])
    zcar[2] = coz[:, 3]
    xcar[0] = jnp.zeros_like(xcar[0])
    xcar[1] = jnp.ones_like(xcar[1])
    xcar[2] = cox[3]
    load.wait(0, 0)

    def first(z, _):
        for h in range(2):
            upsample_part(ebuf0, sbuf0, tab, fine0, h, z)
        return 0

    lax.fori_loop(0, ZG, first, 0)
    bufs = ((ebuf0, sbuf0, fine0, hl0), (ebuf1, sbuf1, fine1, hl1))

    def pair_of_steps(i, _):
        for b in range(2):
            t = i * 2 + b
            k, zg = t // NZG, t % NZG
            other = bufs[1 - b]

            @pl.when(t + 2 < STEPS)
            def _():
                load.start(t + 2, b)

            @pl.when(t + 1 < STEPS)
            def _():
                load.wait(t + 1, 1 - b)

            @pl.when(t >= 3)
            def _():
                for c in stores(t - 3, 1 - b):
                    c.wait()

            def extra(h, z):
                upsample_part(other[0], other[1], tab, other[2], h, z)
                down_part(other[3], down, coarse, eouts[1 - b], souts[1 - b], h, z)

            backward_scan(bufs[b][2], zcar, xcar, coz, cox, bufs[b][3], k, zg, extra)

            @pl.when(t >= 1)
            def _():
                for c in stores(t - 1, 1 - b):
                    c.start()

        return 0

    lax.fori_loop(0, STEPS // 2, pair_of_steps, 0)
    last = (STEPS - 1) % 2
    for c in stores(STEPS - 3, last):
        c.wait()

    def final(z, _):
        for h in range(2):
            down_part(bufs[last][3], down, coarse, eouts[last], souts[last], h, z)
        return 0

    lax.fori_loop(0, ZG, final, 0)
    for c in stores(STEPS - 1, last):
        c.start()
    for t in (STEPS - 2, STEPS - 1):
        for c in stores(t, t % 2):
            c.wait()


def vmem(*shape, dtype=F32):
    return pltpu.VMEM(shape, dtype)


ANY = pl.BlockSpec(memory_space=pl.ANY)
IN_VMEM = pl.BlockSpec(memory_space=pltpu.VMEM)


def local(emission, absorption, target_z, target_x, owner_z, owner_x):
    depth_z, width_x, width_y = absorption.shape
    pixels = 2 * width_y
    count_x = lax.axis_size("gx")
    count_y = lax.axis_size("gy")
    count_z = lax.axis_size("gz")
    ix, iy, iz = lax.axis_index("gx"), lax.axis_index("gy"), lax.axis_index("gz")
    step_z = OPTICAL / (depth_z * count_z)
    step_x = OPTICAL / (width_x * count_x)
    interp = interp_table(width_y)
    rate = interp.T * (-step_z * math.log2(math.e))
    rate_hi = rate.astype(BF16)
    rate_lo = (rate - rate_hi.astype(np.float64)).astype(BF16)
    tab = np.concatenate([interp.T.astype(BF16), rate_hi, rate_lo], axis=0)
    down_e = np.concatenate([interp, interp], axis=0)
    down = np.stack([down_e, down_e * step_z]).astype(BF16)
    e5 = emission.reshape(3, depth_z, NSEG, SEG, width_y)
    s4 = absorption.reshape(depth_z, NSEG, SEG, width_y)

    buffers = [
        vmem(3, ZG, NSEG, HALF, LANE, dtype=BF16), vmem(3, ZG, NSEG, HALF, LANE, dtype=BF16),
        vmem(ZG, NSEG, HALF, LANE, dtype=BF16), vmem(ZG, NSEG, HALF, LANE, dtype=BF16),
        vmem(4, ZG, 2, NSEG * PITCH, LANE), vmem(4, ZG, 2, NSEG * PITCH, LANE),
    ]
    dma = pltpu.SemaphoreType.DMA
    coz, cox, err = pl.pallas_call(
        functools.partial(forward_kernel, 1.0 / step_z, 1.0 / step_x),
        out_shape=[
            jax.ShapeDtypeStruct((SEG, 4, NSEG, 256), F32),
            jax.ShapeDtypeStruct((4, 2, NZ * NSEG, LANE), F32),
            jax.ShapeDtypeStruct((5, 8, LANE), F32),
        ],
        in_specs=[ANY, ANY, ANY, ANY, IN_VMEM],
        out_specs=[IN_VMEM, IN_VMEM, IN_VMEM],
        scratch_shapes=buffers + [
            vmem(SEG, NSEG, 256), vmem(SEG, 4, NSEG, 256), vmem(5, 2, NZ * NSEG, LANE),
            vmem(3, 256, 256, dtype=BF16), vmem(3, NZ, 256, dtype=BF16),
            vmem(3, 2, NSEG * (SEG + 4), LANE), vmem(3, NZ, 256),
            vmem(2, 8, 4, 8, 256), vmem(2, 8, 4, 8, 256), vmem(2, 4, 2, 4, 8, 256), vmem(2, 4, 2, 4, 8, 256),
            vmem(2, 8, 4, 8, 256), vmem(2, 8, 4, 8, 256), vmem(2, 8, 4, 8, 256),
            vmem(4, 4, 8, 256), vmem(4, 4, 8, 256), vmem(4, 4, 8, 256), vmem(4, 4, 8, 256), vmem(NSEG, 8, LANE),
            dma((2, 2)), dma((2,)), dma((2, 2)), dma((2, 3, 2)), dma((2, 3, 2)), dma((2, 2)), dma((3, 2)), dma((3, 2)),
        ],
        compiler_params=pltpu.CompilerParams(
            collective_id=0, has_side_effects=True, vmem_limit_bytes=48 * 2**20
        ),
    )(e5, s4, target_z, target_x, tab)

    labels = jnp.arange(count_x * count_y * count_z, dtype=jnp.int32)
    group_z = count_y * count_z
    rows_z = lax.dynamic_index_in_dim(owner_z[..., 0], ix, 0, keepdims=False)
    rows_z = lax.dynamic_index_in_dim(rows_z, iy, 0, keepdims=False).reshape(NSEG, 2, 2, 4, 2)
    rows_z = lax.dynamic_index_in_dim(rows_z, iz % 2, 2, keepdims=False)
    rows_z = lax.dynamic_index_in_dim(rows_z, iz // 2, 2, keepdims=False)
    own_z = ix * group_z + jnp.transpose(rows_z, (1, 2, 0)).reshape(-1)
    rows_x = lax.dynamic_index_in_dim(owner_x[..., 0], iz, 1, keepdims=False)
    rows_x = lax.dynamic_index_in_dim(rows_x, iy, 0, keepdims=False)
    own_x = lax.dynamic_slice_in_dim(rows_x, ix * 8, 8, 0) * count_z + iz
    own = jnp.concatenate([own_z, own_x])
    tile_err = jnp.sum(err, axis=-1).reshape(-1)
    spread = jnp.sum(jnp.where(own[:, None] == labels[None, :], tile_err[:, None], 0.0), axis=0)
    owned = lax.psum_scatter(spread, ("gx", "gy", "gz"), scatter_dimension=0, tiled=True)
    slots = 2 * width_x // group_z + 2 * depth_z // (count_x * count_y)
    owned_error = (owned / (3.0 * pixels * slots)).reshape(1, 1, 1)

    grad_e, grad_s = pl.pallas_call(
        backward_kernel,
        out_shape=[jax.ShapeDtypeStruct(e5.shape, BF16), jax.ShapeDtypeStruct(s4.shape, BF16)],
        in_specs=[ANY, ANY, IN_VMEM, IN_VMEM, IN_VMEM, IN_VMEM],
        out_specs=[ANY, ANY],
        scratch_shapes=buffers + [
            vmem(4, ZG, HALF // XU, XU * 8, 4 * LANE, dtype=BF16), vmem(4, ZG, HALF // XU, XU * 8, 4 * LANE, dtype=BF16),
            vmem(4, NSEG * PITCH, LANE),
            vmem(3, ZG, NSEG, HALF, LANE, dtype=BF16), vmem(3, ZG, NSEG, HALF, LANE, dtype=BF16),
            vmem(ZG, NSEG, HALF, LANE, dtype=BF16), vmem(ZG, NSEG, HALF, LANE, dtype=BF16),
            vmem(3, SEG, NSEG, 256), vmem(3, 2, NZ * NSEG, LANE),
            dma((2, 2)), dma((2, 2)),
        ],
        compiler_params=pltpu.CompilerParams(vmem_limit_bytes=48 * 2**20),
        cost_estimate=pl.CostEstimate(flops=6 * 10**9, bytes_accessed=20 * 2**20, transcendentals=0),
    )(e5, s4, tab, down, coz, cox)
    return (grad_e.reshape(emission.shape), grad_s.reshape(absorption.shape), owned_error)


def solution(mesh):
    return jax.shard_map(
        local,
        mesh=mesh,
        in_specs=(P(None, "gz", "gx", "gy"), P("gz", "gx", "gy"), P(), P(), P(), P()),
        out_specs=(P(None, "gz", "gx", "gy"), P("gz", "gx", "gy"), P("gx", "gy", "gz")),
        check_vma=False,
    )
```

time: 430 us -> 162 us (0.38); the launches traced: 424 us -> 162 us
  matrix products: 134 us -> 0 us
  local copies, waits for them, and re-layouts: 110 us -> 8.12 us
  Pallas kernels: 0 us -> 85 us
  other arithmetic: 71.6 us -> 0.99 us
  starting transfers between devices: 19.1 us -> 0 us
  waiting for transfers between devices: 14.6 us -> 0 us
  blocking collectives: 70.9 us -> 65.5 us
    dot_general x8 -> x0, matrix products: 134 us -> none  [the longest x2 53.7 us: prefix_along(): return jnp.einsum('kj,jab->kab', summing, sample_values, precision=HIGHEST)]
    pallas_call x0 -> x2, Pallas kernels: none -> 85 us  [the longest x1 44.3 us: local(): pl.pallas_call(functools.partial(forward_kernel, 1.0 / step_z, 1.0 / step...]
    reduce_sum x5 -> x2, other arithmetic: 35.9 us -> 0.17 us  [the longest x1 0.09 us: local(): jnp.sum(jnp.where(own[:, None] == labels[None, :], tile_err[:, None], 0.0...]
    reshape x1, local copies, waits for them, and re-layouts: 24.7 us -> 0.16 us  [local(): lax.dynamic_index_in_dim(rows_z, iy, 0, keepdims=False)]
    mul x3 -> x0, local copies, waits for them, and re-layouts: 21.4 us -> none  [the longest x2 21.4 us: local_forward(): optical = march_step * sigma_up]
    dot_general x2 -> x0, local copies, waits for them, and re-layouts: 20.8 us -> none  [prefix_along(): return jnp.einsum('kj,ajb->akb', summing, sample_values, precision=HIGHEST)]
    all_to_all x4 -> x0, starting transfers between devices: 19.1 us -> none  [the longest x1 6.39 us: local(): lax.all_to_all(footprint_z, 'gz', split_axis=2, concat_axis=1, tiled=True)]
    mul x17 -> x0, other arithmetic: 17.2 us -> none  [the longest x1 14.1 us: local_backward(): behind = prefix_along(shares * inner_sum, axis, True)]
  transfers between devices with their start and end apart: 4 -> 0, of which waited for: 2 -> 0; matrix products, arithmetic and copies ran while one was open for 4% -> 0% of each run, Pallas kernels for 0% -> 0%
where the time goes in v1:
time: 162 us
  Pallas kernels  85 us (52%)
  blocking collectives  65.5 us (40%)
  local copies, waits for them, and re-layouts  8.12 us (5%)
  between operations  2.54 us (2%)
    unnamed x1, blocking collectives  65.5 us
    pallas_call x1, Pallas kernels, local(): pl.pallas_call(functools.partial(forward_kernel, 1.0 / step_z, 1.0 / step...  44.3 us
    pallas_call x1, Pallas kernels, local(): pl.pallas_call(backward_kernel, out_shape=[jax.ShapeDtypeStruct(e5.shape,...  40.7 us
    unnamed x20, local copies, waits for them, and re-layouts  7.75 us

profile of v1, /device:TPU:1, one launch (start us, length us, event | category | flops | bytes accessed | tf_op | source)
XLA Modules:
  0.0 162.1 jit_solution(13948733588510360431)
XLA Ops:
  0.6 0.0 copy-start
  0.7 0.7 fusion.2
  1.4 0.0 copy-done
  1.5 0.2 reshape.51
  1.6 0.1 copy.15
  1.7 0.1 add.82
  1.8 0.1 pad_add_fusion
  1.9 0.0 copy-start.1
  1.9 1.6 copy-done.1
  3.5 0.0 copy-start.3
  3.5 1.4 copy-done.3
  4.9 0.0 copy-start.4
  4.9 0.9 copy-done.4
  5.8 0.0 copy-start.2
  5.8 0.0 copy-start.5
  5.8 44.3 %shard_map.103 = (f32[32,4,8,256]{3,2,1,0:T(8,128)S(1)}, f32[4,2,256,128]{3,2,1,0:T(8,128)S(1)}, f32[5,8,128]{2,1,0:T(8,128)S(1)}) custom-call(bf16[3,32,8,32,128]{4,3,2,1,0:T(8,128)(2,1)} %bitcast.13, bf16[32,8,32,128]{3,2,1,0:T(8,128)(2,1)S(1)} %bitcast.11, bf16[3,1024,1024]{2,1,0:T(8,128)(2,1)} %tz_hbm.1, bf16[3,256,1024]{2,1,0:T(8,128)(2,1)S(1)} %copy-done.3, ...), custom_call_target="tpu_custom_call" | custom-call | tf_op jit(solution)/shard_map/pallas_call | solution.py:599
  50.2 0.0 copy-start.6
  50.2 1.0 copy-done.6
  51.1 0.1 reduce_sum.18
  51.2 0.1 broadcast_in_dim.16
  51.3 0.1 select_reduce_fusion
  51.4 65.5 %all-reduce = f32[128]{0:T(128)S(1)} all-reduce(f32[128]{0:T(128)S(1)} %select_reduce_fusion), channel_id=2, replica_groups=mesh['gx'=4,'gy'=4,'gz'=8] {'gx','gy','gz'}, use_global_device_ids=true, to_apply=%region_2.3.clone | all-reduce | flops 128 | bytes 1024
  116.8 0.6 dynamic-slice.10
  118.1 0.0 copy-done.2
  118.1 0.0 copy-done.5
  118.1 0.0 copy-start.7
  118.1 1.2 copy-done.7
  119.3 0.0 copy-start.8
  119.3 0.9 copy-done.8
  120.3 40.7 %shard_map.104 = (bf16[3,32,8,32,128]{4,3,2,1,0:T(8,128)(2,1)}, bf16[32,8,32,128]{3,2,1,0:T(8,128)(2,1)}) custom-call(bf16[3,32,8,32,128]{4,3,2,1,0:T(8,128)(2,1)} %bitcast.14, bf16[32,8,32,128]{3,2,1,0:T(8,128)(2,1)S(1)} %bitcast.12, bf16[384,256]{1,0:T(8,128)(2,1)S(1)} %copy-done.5, bf16[2,512,128]{2,1,0:T(8,128)(2,1)S(1)} %copy-done.8, ...), custom_call_target="tpu_custom_call" | custom-call | flops 6000000000 | bytes 20971520 | tf_op jit(solution)/shard_map/pallas_call | solution.py:639
  (3 shorter events, 0.0 us)
Async XLA Ops:
  0.6 0.8 copy-start
  1.9 1.6 copy-start.1
  3.5 1.4 copy-start.3
  4.9 0.9 copy-start.4
  5.8 112.2 %copy-start.2 = (bf16[32,256,128]{2,1,0:T(8,128)(2,1)S(1)}, bf16[32,256,128]{2,1,0:T(8,128)(2,1)}, u32[]{:S(2)}) copy-start(bf16[32,256,128]{2,1,0:T(8,128)(2,1)} %param.9) | copy-start | bytes 6291460
  5.8 112.2 %copy-start.5 = (bf16[384,256]{1,0:T(8,128)(2,1)S(1)}, bf16[384,256]{1,0:T(8,128)(2,1)}, u32[]{:S(2)}) copy-start(bf16[384,256]{1,0:T(8,128)(2,1)} %constant.169.clone.tab) | copy-start | bytes 589828
  50.2 1.0 copy-start.6
  118.1 1.2 copy-start.7
  119.3 0.9 copy-start.8

commit v2 on v1

--- a/solution.py
+++ b/solution.py
@@ -22,7 +22,6 @@
 NZ = 32
 NZG = NZ // ZG
 STEPS = 2 * NZG
-XU = 4
 LANE = 128
 
 
@@ -44,19 +43,22 @@
             fine[f, z, h, s * PITCH : s * PITCH + HALF] = r[s * HALF : (s + 1) * HALF, half(h)]
 
 
-def upsample_part(ebuf, sbuf, tab, fine, h, z):
+def upsample_part(ebuf, sbuf, tab, fine, part):
     rows = NSEG * HALF
-    if h == 0:
-        a = jnp.concatenate([ebuf[0, z].reshape(rows, LANE), ebuf[1, z].reshape(rows, LANE)], axis=0)
+    if part == 0:
+        a = ebuf[0:2].reshape(2 * ZG * rows, LANE)
         r = jnp.dot(a, tab[0:LANE], preferred_element_type=F32)
-        upsample_store(fine, 0, z, r[:rows])
-        upsample_store(fine, 1, z, r[rows:])
+        for f in range(2):
+            for z in range(ZG):
+                i = f * ZG + z
+                upsample_store(fine, f, z, r[i * rows : (i + 1) * rows])
     else:
-        r = jnp.dot(ebuf[2, z].reshape(rows, LANE), tab[0:LANE], preferred_element_type=F32)
-        upsample_store(fine, 2, z, r)
-        s = sbuf[z].reshape(rows, LANE)
-        r = jnp.dot(jnp.concatenate([s, s], axis=1), tab[LANE:], preferred_element_type=F32)
-        upsample_store(fine, 3, z, r)
+        r = jnp.dot(ebuf[2].reshape(ZG * rows, LANE), tab[0:LANE], preferred_element_type=F32)
+        s = sbuf[...].reshape(ZG * rows, LANE)
+        q = jnp.dot(jnp.concatenate([s, s], axis=1), tab[LANE:], preferred_element_type=F32)
+        for z in range(ZG):
+            upsample_store(fine, 2, z, r[z * rows : (z + 1) * rows])
+            upsample_store(fine, 3, z, q[z * rows : (z + 1) * rows])
 
 
 class Loader:
@@ -85,36 +87,29 @@
     for h in range(2):
         hs = half(h)
         rows = [pl.ds(pl.multiple_of((zg * ZG + z) * NSEG, NSEG), NSEG) for z in range(ZG)]
-        start = tuple(xc[i, h, rows[z], :] for z in range(ZG) for i in range(5))
-
-        def step(j, carry):
-            carry = list(carry)
-            extra(h, j)
-            for u in range(XU):
-                xm = j * XU + u
-                zr = k * HALF + xm
-                s_z = zs[zr, :, hs]
-                c0, c1, c2, t_z = [zc[zr, i, :, hs] for i in range(4)]
-                for z in range(ZG):
-                    e0, e1, e2, sg = [fine[f, z, h, pl.ds(xm, NSEG, stride=PITCH), :] for f in range(4)]
-                    s_z = s_z + sg
-                    t_new = jnp.exp2(s_z)
-                    share = t_z - t_new
-                    t_z = t_new
-                    c0 = c0 + share * e0
-                    c1 = c1 + share * e1
-                    c2 = c2 + share * e2
-                    s_x, t_x, d0, d1, d2 = carry[z * 5 : z * 5 + 5]
-                    s_x = s_x + sg
-                    t_new = jnp.exp2(s_x * 0.25)
-                    share = t_x - t_new
-                    carry[z * 5 : z * 5 + 5] = [s_x, t_new, d0 + share * e0, d1 + share * e1, d2 + share * e2]
-                zs[zr, :, hs] = s_z
-                for i, v in enumerate((c0, c1, c2, t_z)):
-                    zc[zr, i, :, hs] = v
-            return tuple(carry)
-
-        carry = lax.fori_loop(0, HALF // XU, step, start)
+        carry = [xc[i, h, rows[z], :] for z in range(ZG) for i in range(5)]
+        extra(h)
+        for xm in range(HALF):
+            zr = k * HALF + xm
+            s_z = zs[zr, :, hs]
+            c0, c1, c2, t_z = [zc[zr, i, :, hs] for i in range(4)]
+            for z in range(ZG):
+                e0, e1, e2, sg = [fine[f, z, h, pl.ds(xm, NSEG, stride=PITCH), :] for f in range(4)]
+                s_z = s_z + sg
+                t_new = jnp.exp2(s_z)
+                share = t_z - t_new
+                t_z = t_new
+                c0 = c0 + share * e0
+                c1 = c1 + share * e1
+                c2 = c2 + share * e2
+                s_x, t_x, d0, d1, d2 = carry[z * 5 : z * 5 + 5]
+                s_x = s_x + sg
+                t_new = jnp.exp2(s_x * 0.25)
+                share = t_x - t_new
+                carry[z * 5 : z * 5 + 5] = [s_x, t_new, d0 + share * e0, d1 + share * e1, d2 + share * e2]
+            zs[zr, :, hs] = s_z
+            for i, v in enumerate((c0, c1, c2, t_z)):
+                zc[zr, i, :, hs] = v
         for z in range(ZG):
             for i in range(5):
                 xc[i, h, rows[z], :] = carry[z * 5 + i]
@@ -145,14 +140,15 @@
 
 
 def forward_kernel(
-    inv_z, inv_x,
-    e_hbm, s_hbm, tz_hbm, tx_hbm, tab,
-    coz, cox, err,
+    inv_z, inv_x, share,
+    e_hbm, s_hbm, tz_hbm, tx_hbm, oz_hbm, ox_hbm, tab_hbm, perm_hbm,
+    coz, cox, owned,
     ebuf0, ebuf1, sbuf0, sbuf1, fine0, fine1, zs, zc, xc,
     tzb, txb, tzf, txf,
     sib, pc, got, rep, back, fin, finr,
     xloc, xgot, xrep, xback, xsuf,
-    in_sem, t_sem, sem_sib, sem_chip, sem_rep, sem_fin, sem_x, sem_xr,
+    tab, perm, err, ozb, oxb, ez, ex, ey,
+    in_sem, t_sem, sem_sib, sem_chip, sem_rep, sem_fin, sem_x, sem_xr, sem_ez, sem_ex, sem_ey,
 ):
     ix, iy, iz = lax.axis_index("gx"), lax.axis_index("gy"), lax.axis_index("gz")
     chip, core = iz // 2, iz % 2
@@ -162,14 +158,22 @@
     px = pl.ds(pl.multiple_of(iy * 256, 256), 256)
     tz_copy = pltpu.make_async_copy(tz_hbm.at[:, pl.ds(pl.multiple_of(ix * 256, 256), 256), px], tzb, t_sem.at[0])
     tx_copy = pltpu.make_async_copy(tx_hbm.at[:, pl.ds(pl.multiple_of(iz * NZ, NZ), NZ), px], txb, t_sem.at[1])
-    tz_copy.start()
-    tx_copy.start()
+    oz_copy = pltpu.make_async_copy(oz_hbm.at[ix, iy], ozb, t_sem.at[2])
+    ox_copy = pltpu.make_async_copy(ox_hbm.at[iy, iz], oxb, t_sem.at[3])
+    tab_copy = pltpu.make_async_copy(tab_hbm, tab, t_sem.at[4])
+    perm_copy = pltpu.make_async_copy(perm_hbm, perm, t_sem.at[5])
+    tab_copy.start()
+    late = (tz_copy, tx_copy, oz_copy, ox_copy, perm_copy)
+    for c in late:
+        c.start()
 
     sibling = {"gz": chip * 2 + 1 - core}
     chips = [{"gz": lax.rem(chip + d, 4) * 2 + core} for d in (1, 2, 3)]
     slabs = [{"gx": lax.rem(ix + d, 4)} for d in (1, 2, 3)]
     barrier = pltpu.get_barrier_semaphore()
-    for peer in [sibling] + chips + slabs:
+    row = [{"gz": lax.rem(iz + d, 8)} for d in range(1, 8)]
+    column = [{"gy": lax.rem(iy + d, 4)} for d in (1, 2, 3)]
+    for peer in row + slabs + column:
         pl.semaphore_signal(barrier, inc=1, device_id=peer, device_id_type=pl.DeviceIdType.MESH)
 
     def remote(src, dst, sems, peer):
@@ -322,6 +326,54 @@
                     cox[3, h, rows, :] = -(front * xsuf[s])
                     front = front * xc[1, h, rows, :]
 
+    lane = lax.broadcasted_iota(jnp.int32, (8, LANE), 1)
+    sub = lax.broadcasted_iota(jnp.int32, (8, LANE), 0)
+
+    def scatter(sq, ids):
+        owner = jnp.zeros((8, LANE), jnp.int32)
+        for s, o in enumerate(ids):
+            owner = jnp.where(sub == s, o, owner)
+        return jnp.where(lane == owner, jnp.sum(sq, axis=1, keepdims=True), 0.0)
+
+    def ez_copies():
+        return [remote(ez.at[7], ez.at[d - 1], sem_ez.at[d - 1], row[d - 1]) for d in range(1, 8)]
+
+    def ex_copies():
+        return [remote(ex.at[3], ex.at[d - 1], sem_ex.at[d - 1], slabs[d - 1]) for d in (1, 2, 3)]
+
+    def ey_copies():
+        return [remote(ey.at[3], ey.at[d - 1], sem_ey.at[d - 1], column[d - 1]) for d in (1, 2, 3)]
+
+    def err_start():
+        total = jnp.zeros((8, LANE), F32)
+        for k in range(2):
+            for i in range(2):
+                cell = k * HALF + core * 8 + chip * 2 + i
+                total = total + scatter(err[k * 2 + i], [ix * 32 + ozb[0, s * SEG + cell] for s in range(NSEG)])
+        ez[7] = total
+        ex[3] = scatter(err[4], [oxb[0, ix * 8 + s] * 8 + iz for s in range(8)])
+        for c in ez_copies() + ex_copies():
+            c.start()
+
+    def err_middle():
+        for c in ez_copies() + ex_copies():
+            c.wait_recv()
+        total = ez[7] + ex[3]
+        for d in range(7):
+            total = total + ez[d]
+        for d in range(3):
+            total = total + ex[d]
+        ey[3] = total
+        for c in ey_copies():
+            c.start()
+
+    def err_finish():
+        for c in ey_copies():
+            c.wait_recv()
+        total = ey[0] + ey[1] + ey[2] + ey[3]
+        mine = jnp.where(lane == ix * 32 + iy * 8 + iz, total, 0.0)
+        owned[0, 0] = jnp.sum(mine) * share
+
     zs[...] = jnp.zeros_like(zs)
     xc[0] = jnp.zeros_like(xc[0])
     xc[1] = jnp.ones_like(xc[1])
@@ -335,13 +387,9 @@
 
     lax.fori_loop(0, SEG, clear, 0)
     load.wait(0, 0)
-
-    def first(z, _):
-        for h in range(2):
-            upsample_part(ebuf0, sbuf0, tab, fine0, h, z)
-        return 0
-
-    lax.fori_loop(0, ZG, first, 0)
+    tab_copy.wait()
+    for part in range(2):
+        upsample_part(ebuf0, sbuf0, tab, fine0, part)
 
     bufs = ((ebuf0, sbuf0, fine0), (ebuf1, sbuf1, fine1))
 
@@ -361,15 +409,15 @@
 
             forward_scan(
                 bufs[b][2], zs, zc, xc, k, zg,
-                lambda h, z: upsample_part(other[0], other[1], tab, other[2], h, z),
+                lambda part: upsample_part(other[0], other[1], tab, other[2], part),
             )
 
         @pl.when(i == 3)
         def _():
-            pl.semaphore_wait(barrier, 7)
+            pl.semaphore_wait(barrier, 13)
             sib_copy(0).start()
 
-        @pl.when(i == 5)
+        @pl.when(i == 4)
         def _():
             z_compose(0)
 
@@ -378,14 +426,15 @@
     lax.fori_loop(0, STEPS // 2, pair_of_steps, 0)
     sib_copy(1).start()
     x_compose()
-    tz_copy.wait()
-    tx_copy.wait()
+    for c in late:
+        c.wait()
 
     def widen(c, _):
+        r = jnp.dot(tzb[c], perm[...], preferred_element_type=F32)
         for h in range(2):
             for s in range(NSEG):
-                tzf[c, h, pl.ds(s * (SEG + 4), SEG), :] = tzb[c, pl.ds(s * SEG, SEG), half(h)].astype(F32)
-        txf[c] = txb[c].astype(F32)
+                tzf[c, h, pl.ds(s * (SEG + 4), SEG), :] = r[s * SEG : (s + 1) * SEG, half(h)]
+        txf[c] = jnp.dot(txb[c], perm[...], preferred_element_type=F32)
         return 0
 
     lax.fori_loop(0, 3, widen, 0)
@@ -393,97 +442,95 @@
     z_compose(1)
     x_merge()
     z_split(0)
+    z_merge(1)
+    err_start()
     x_split()
-    z_merge(1)
     z_finish(0)
     z_split(1)
+    err_middle()
     z_finish(1)
+    err_finish()
     for k in range(2):
         for c in [sib_copy(k)] + chip_copies(k) + rep_copies(k) + [fin_copy(k)]:
             c.wait_send()
-    for c in x_copies() + xr_copies():
+    for c in x_copies() + xr_copies() + ez_copies() + ex_copies() + ey_copies():
         c.wait_send()
 
 
-def backward_scan(fine, zcar, xcar, coz, cox, hl, k, zg, extra):
-    for h in range(2):
-        hs = half(h)
-        rows = [pl.ds(pl.multiple_of((zg * ZG + z) * NSEG, NSEG), NSEG) for z in range(ZG)]
-        start = tuple(xcar[i, h, rows[z], :] for z in range(ZG) for i in range(3))
-        gx = [[cox[c, h, rows[z], :] for c in range(3)] for z in range(ZG)]
-
-        def step(j, carry):
-            carry = list(carry)
-            extra(h, j)
-            held = [[[None] * XU for _ in range(4)] for _ in range(ZG)]
-            for u in range(XU):
-                xm = j * XU + u
-                zr = k * HALF + xm
-                s_z, t_z, a_z = [zcar[i, zr, :, hs] for i in range(3)]
-                g0, g1, g2 = [coz[zr, c, :, hs] for c in range(3)]
-                for z in range(ZG):
-                    e0, e1, e2, sg = [fine[f, z, h, pl.ds(xm, NSEG, stride=PITCH), :] for f in range(4)]
-                    s_z = s_z + sg
-                    t_new = jnp.exp2(s_z)
-                    share_z = t_z - t_new
-                    t_z = t_new
-                    inner = g0 * e0 + g1 * e1 + g2 * e2
-                    a_z = a_z + share_z * inner
-                    grad = t_new * inner + a_z
-                    h0, h1, h2 = gx[z]
-                    s_x, t_x, a_x = carry[z * 3 : z * 3 + 3]
-                    s_x = s_x + sg
-                    t_new = jnp.exp2(s_x * 0.25)
-                    share_x = t_x - t_new
-                    inner = h0 * e0 + h1 * e1 + h2 * e2
-                    a_x = a_x + share_x * inner
-                    grad = grad + 0.25 * (t_new * inner + a_x)
-                    carry[z * 3 : z * 3 + 3] = [s_x, t_new, a_x]
-                    held[z][0][u] = g0 * share_z + h0 * share_x
-                    held[z][1][u] = g1 * share_z + h1 * share_x
-                    held[z][2][u] = g2 * share_z + h2 * share_x
-                    held[z][3][u] = grad
-                for i, v in enumerate((s_z, t_z, a_z)):
-                    zcar[i, zr, :, hs] = v
-                if u % 2:
-                    for z in range(ZG):
-                        for f in range(4):
-                            v = jnp.concatenate(held[z][f][u - 1 : u + 1], axis=0)
-                            hi = v.astype(BF16)
-                            lo = (v - hi.astype(F32)).astype(BF16)
-                            r = slice((u - 1) * 8, (u + 1) * 8)
-                            hl[f, z, j, r, h * LANE : (h + 1) * LANE] = hi
-                            hl[f, z, j, r, (h + 2) * LANE : (h + 3) * LANE] = lo
-            return tuple(carry)
-
-        carry = lax.fori_loop(0, HALF // XU, step, start)
-        for z in range(ZG):
+def project_down(even, odd, first, last, near, far):
+    side = jnp.where(first, even, pltpu.roll(odd, 1, axis=1)) + jnp.where(last, odd, pltpu.roll(even, LANE - 1, axis=1))
+    return near * (even + odd) + (side if far is None else far * side)
+
+
+def backward_scan(fine, zcar, xcar, coz, cox, coarse, k, zg, pair, far):
+    lanes = lax.broadcasted_iota(jnp.int32, (NSEG, LANE), 1)
+    first, last = lanes == 0, lanes == LANE - 1
+    planes = [pair * 2 + i for i in range(2)]
+    rows = [pl.ds(pl.multiple_of((zg * ZG + z) * NSEG, NSEG), NSEG) for z in planes]
+    carry = [[[xcar[i, h, r, :] for i in range(3)] for h in range(2)] for r in rows]
+    gx = [[[cox[c, h, r, :] for c in range(3)] for h in range(2)] for r in rows]
+    for xm in range(HALF):
+        zr = k * HALF + xm
+        z_carry = [[zcar[i, zr, :, half(h)] for i in range(3)] for h in range(2)]
+        gz = [[coz[zr, c, :, half(h)] for c in range(3)] for h in range(2)]
+        for n, z in enumerate(planes):
+            out = [[None] * 2 for _ in range(4)]
+            for h in range(2):
+                e0, e1, e2, sg = [fine[f, z, h, pl.ds(xm, NSEG, stride=PITCH), :] for f in range(4)]
+                g0, g1, g2 = gz[h]
+                s_z, t_z, a_z = z_carry[h]
+                s_z = s_z + sg
+                t_new = jnp.exp2(s_z)
+                share_z = t_z - t_new
+                inner = g0 * e0 + g1 * e1 + g2 * e2
+                a_z = a_z + share_z * inner
+                grad = t_new * inner + a_z
+                z_carry[h] = [s_z, t_new, a_z]
+                h0, h1, h2 = gx[n][h]
+                s_x, t_x, a_x = carry[n][h]
+                s_x = s_x + sg
+                t_new = jnp.exp2(s_x * 0.25)
+                share_x = t_x - t_new
+                inner = h0 * e0 + h1 * e1 + h2 * e2
+                a_x = a_x + share_x * inner
+                out[3][h] = grad + 0.25 * (t_new * inner + a_x)
+                carry[n][h] = [s_x, t_new, a_x]
+                out[0][h] = g0 * share_z + h0 * share_x
+                out[1][h] = g1 * share_z + h1 * share_x
+                out[2][h] = g2 * share_z + h2 * share_x
+            for f in range(4):
+                v = project_down(out[f][0], out[f][1], first, last, 3.0 * far if f == 3 else 3.0, far if f == 3 else None)
+                coarse[f, z, pl.ds(xm, NSEG, stride=PITCH), :] = v
+        for h in range(2):
             for i in range(3):
-                xcar[i, h, rows[z], :] = carry[z * 3 + i]
-
-
-def down_part(hl, down, coarse, eout, sout, h, z):
-    rows = NSEG * HALF
-    for f in ((0, 1) if h == 0 else (2, 3)):
-        a = hl[f, z].reshape(rows, 4 * LANE)
-        r = jnp.dot(a, down[int(f == 3)], preferred_element_type=F32)
-        for m in range(HALF):
-            coarse[f, pl.ds(m, NSEG, stride=PITCH), :] = r[m * 8 : (m + 1) * 8]
-        for s in range(NSEG):
-            v = coarse[f, pl.ds(s * PITCH, HALF), :].astype(BF16)
-            if f == 3:
-                sout[z, s] = v
-            else:
-                eout[f, z, s] = v
+                zcar[i, zr, :, half(h)] = z_carry[h][i]
+    for n, r in enumerate(rows):
+        for h in range(2):
+            for i in range(3):
+                xcar[i, h, r, :] = carry[n][h][i]
+
+
+def narrow_part(coarse, eout, sout, part):
+    for z in (2 * part, 2 * part + 1):
+        for f in range(4):
+            for s in range(NSEG):
+                v = coarse[f, z, pl.ds(s * PITCH, HALF), :].astype(BF16)
+                if f == 3:
+                    sout[z, s] = v
+                else:
+                    eout[f, z, s] = v
 
 
 def backward_kernel(
-    e_hbm, s_hbm, tab, down, coz, cox,
+    far,
+    e_hbm, s_hbm, tab_hbm, coz, cox,
     ge_hbm, gs_hbm,
-    ebuf0, ebuf1, sbuf0, sbuf1, fine0, fine1, hl0, hl1, coarse,
+    ebuf0, ebuf1, sbuf0, sbuf1, fine0, fine1, tab, coarse0, coarse1,
     eout0, eout1, sout0, sout1, zcar, xcar,
-    in_sem, out_sem,
+    in_sem, out_sem, tab_sem,
 ):
+    tab_copy = pltpu.make_async_copy(tab_hbm, tab, tab_sem)
+    tab_copy.start()
     load = Loader(e_hbm, s_hbm, (ebuf0, ebuf1), (sbuf0, sbuf1), in_sem)
     load.start(0, 0)
     load.start(1, 1)
@@ -504,14 +551,10 @@
     xcar[1] = jnp.ones_like(xcar[1])
     xcar[2] = cox[3]
     load.wait(0, 0)
-
-    def first(z, _):
-        for h in range(2):
-            upsample_part(ebuf0, sbuf0, tab, fine0, h, z)
-        return 0
-
-    lax.fori_loop(0, ZG, first, 0)
-    bufs = ((ebuf0, sbuf0, fine0, hl0), (ebuf1, sbuf1, fine1, hl1))
+    tab_copy.wait()
+    for part in range(2):
+        upsample_part(ebuf0, sbuf0, tab, fine0, part)
+    bufs = ((ebuf0, sbuf0, fine0, coarse0), (ebuf1, sbuf1, fine1, coarse1))
 
     def pair_of_steps(i, _):
         for b in range(2):
@@ -532,11 +575,10 @@
                 for c in stores(t - 3, 1 - b):
                     c.wait()
 
-            def extra(h, z):
-                upsample_part(other[0], other[1], tab, other[2], h, z)
-                down_part(other[3], down, coarse, eouts[1 - b], souts[1 - b], h, z)
-
-            backward_scan(bufs[b][2], zcar, xcar, coz, cox, bufs[b][3], k, zg, extra)
+            for part in range(2):
+                upsample_part(other[0], other[1], tab, other[2], part)
+                narrow_part(other[3], eouts[1 - b], souts[1 - b], part)
+                backward_scan(bufs[b][2], zcar, xcar, coz, cox, bufs[b][3], k, zg, part, far)
 
             @pl.when(t >= 1)
             def _():
@@ -549,13 +591,8 @@
     last = (STEPS - 1) % 2
     for c in stores(STEPS - 3, last):
         c.wait()
-
-    def final(z, _):
-        for h in range(2):
-            down_part(bufs[last][3], down, coarse, eouts[last], souts[last], h, z)
-        return 0
-
-    lax.fori_loop(0, ZG, final, 0)
+    for part in range(2):
+        narrow_part(bufs[last][3], eouts[last], souts[last], part)
     for c in stores(STEPS - 1, last):
         c.start()
     for t in (STEPS - 2, STEPS - 1):
@@ -567,7 +604,7 @@
     return pltpu.VMEM(shape, dtype)
 
 
-ANY = pl.BlockSpec(memory_space=pl.ANY)
+HBM = pl.BlockSpec(memory_space=pltpu.HBM)
 IN_VMEM = pl.BlockSpec(memory_space=pltpu.VMEM)
 
 
@@ -577,16 +614,16 @@
     count_x = lax.axis_size("gx")
     count_y = lax.axis_size("gy")
     count_z = lax.axis_size("gz")
-    ix, iy, iz = lax.axis_index("gx"), lax.axis_index("gy"), lax.axis_index("gz")
     step_z = OPTICAL / (depth_z * count_z)
     step_x = OPTICAL / (width_x * count_x)
     interp = interp_table(width_y)
     rate = interp.T * (-step_z * math.log2(math.e))
+    order = np.concatenate([np.arange(0, pixels, 2), np.arange(1, pixels, 2)])
     rate_hi = rate.astype(BF16)
     rate_lo = (rate - rate_hi.astype(np.float64)).astype(BF16)
-    tab = np.concatenate([interp.T.astype(BF16), rate_hi, rate_lo], axis=0)
-    down_e = np.concatenate([interp, interp], axis=0)
-    down = np.stack([down_e, down_e * step_z]).astype(BF16)
+    tab = np.concatenate([interp.T.astype(BF16), rate_hi, rate_lo], axis=0)[:, order]
+    perm = np.eye(pixels)[:, order].astype(BF16)
+    slots = 2 * width_x // (count_y * count_z) + 2 * depth_z // (count_x * count_y)
     e5 = emission.reshape(3, depth_z, NSEG, SEG, width_y)
     s4 = absorption.reshape(depth_z, NSEG, SEG, width_y)
 
@@ -596,15 +633,15 @@
         vmem(4, ZG, 2, NSEG * PITCH, LANE), vmem(4, ZG, 2, NSEG * PITCH, LANE),
     ]
     dma = pltpu.SemaphoreType.DMA
-    coz, cox, err = pl.pallas_call(
-        functools.partial(forward_kernel, 1.0 / step_z, 1.0 / step_x),
+    coz, cox, owned = pl.pallas_call(
+        functools.partial(forward_kernel, 0.25 / step_z, 0.25 / step_x, 1.0 / (3.0 * pixels * slots)),
         out_shape=[
             jax.ShapeDtypeStruct((SEG, 4, NSEG, 256), F32),
             jax.ShapeDtypeStruct((4, 2, NZ * NSEG, LANE), F32),
-            jax.ShapeDtypeStruct((5, 8, LANE), F32),
+            jax.ShapeDtypeStruct((1, 1), F32),
         ],
-        in_specs=[ANY, ANY, ANY, ANY, IN_VMEM],
-        out_specs=[IN_VMEM, IN_VMEM, IN_VMEM],
+        in_specs=[HBM] * 8,
+        out_specs=[IN_VMEM, IN_VMEM, pl.BlockSpec(memory_space=pltpu.SMEM)],
         scratch_shapes=buffers + [
             vmem(SEG, NSEG, 256), vmem(SEG, 4, NSEG, 256), vmem(5, 2, NZ * NSEG, LANE),
             vmem(3, 256, 256, dtype=BF16), vmem(3, NZ, 256, dtype=BF16),
@@ -612,47 +649,36 @@
             vmem(2, 8, 4, 8, 256), vmem(2, 8, 4, 8, 256), vmem(2, 4, 2, 4, 8, 256), vmem(2, 4, 2, 4, 8, 256),
             vmem(2, 8, 4, 8, 256), vmem(2, 8, 4, 8, 256), vmem(2, 8, 4, 8, 256),
             vmem(4, 4, 8, 256), vmem(4, 4, 8, 256), vmem(4, 4, 8, 256), vmem(4, 4, 8, 256), vmem(NSEG, 8, LANE),
-            dma((2, 2)), dma((2,)), dma((2, 2)), dma((2, 3, 2)), dma((2, 3, 2)), dma((2, 2)), dma((3, 2)), dma((3, 2)),
+            vmem(3 * LANE, 256, dtype=BF16), vmem(256, 256, dtype=BF16), vmem(5, 8, LANE),
+            pltpu.SMEM((1, 256), jnp.int32), pltpu.SMEM((1, NZ), jnp.int32),
+            vmem(8, 8, LANE), vmem(4, 8, LANE), vmem(4, 8, LANE),
+            dma((2, 2)), dma((6,)), dma((2, 2)), dma((2, 3, 2)), dma((2, 3, 2)), dma((2, 2)), dma((3, 2)), dma((3, 2)),
+            dma((7, 2)), dma((3, 2)), dma((3, 2)),
         ],
         compiler_params=pltpu.CompilerParams(
             collective_id=0, has_side_effects=True, vmem_limit_bytes=48 * 2**20
         ),
-    )(e5, s4, target_z, target_x, tab)
-
-    labels = jnp.arange(count_x * count_y * count_z, dtype=jnp.int32)
-    group_z = count_y * count_z
-    rows_z = lax.dynamic_index_in_dim(owner_z[..., 0], ix, 0, keepdims=False)
-    rows_z = lax.dynamic_index_in_dim(rows_z, iy, 0, keepdims=False).reshape(NSEG, 2, 2, 4, 2)
-    rows_z = lax.dynamic_index_in_dim(rows_z, iz % 2, 2, keepdims=False)
-    rows_z = lax.dynamic_index_in_dim(rows_z, iz // 2, 2, keepdims=False)
-    own_z = ix * group_z + jnp.transpose(rows_z, (1, 2, 0)).reshape(-1)
-    rows_x = lax.dynamic_index_in_dim(owner_x[..., 0], iz, 1, keepdims=False)
-    rows_x = lax.dynamic_index_in_dim(rows_x, iy, 0, keepdims=False)
-    own_x = lax.dynamic_slice_in_dim(rows_x, ix * 8, 8, 0) * count_z + iz
-    own = jnp.concatenate([own_z, own_x])
-    tile_err = jnp.sum(err, axis=-1).reshape(-1)
-    spread = jnp.sum(jnp.where(own[:, None] == labels[None, :], tile_err[:, None], 0.0), axis=0)
-    owned = lax.psum_scatter(spread, ("gx", "gy", "gz"), scatter_dimension=0, tiled=True)
-    slots = 2 * width_x // group_z + 2 * depth_z // (count_x * count_y)
-    owned_error = (owned / (3.0 * pixels * slots)).reshape(1, 1, 1)
+    )(
+        e5, s4, target_z, target_x, owner_z.reshape(count_x, count_y, 1, width_x),
+        owner_x.reshape(count_y, count_z, 1, depth_z), tab, perm,
+    )
 
     grad_e, grad_s = pl.pallas_call(
-        backward_kernel,
+        functools.partial(backward_kernel, step_z),
         out_shape=[jax.ShapeDtypeStruct(e5.shape, BF16), jax.ShapeDtypeStruct(s4.shape, BF16)],
-        in_specs=[ANY, ANY, IN_VMEM, IN_VMEM, IN_VMEM, IN_VMEM],
-        out_specs=[ANY, ANY],
+        in_specs=[HBM, HBM, HBM, IN_VMEM, IN_VMEM],
+        out_specs=[HBM, HBM],
         scratch_shapes=buffers + [
-            vmem(4, ZG, HALF // XU, XU * 8, 4 * LANE, dtype=BF16), vmem(4, ZG, HALF // XU, XU * 8, 4 * LANE, dtype=BF16),
-            vmem(4, NSEG * PITCH, LANE),
+            vmem(3 * LANE, 256, dtype=BF16), vmem(4, ZG, NSEG * PITCH, LANE), vmem(4, ZG, NSEG * PITCH, LANE),
             vmem(3, ZG, NSEG, HALF, LANE, dtype=BF16), vmem(3, ZG, NSEG, HALF, LANE, dtype=BF16),
             vmem(ZG, NSEG, HALF, LANE, dtype=BF16), vmem(ZG, NSEG, HALF, LANE, dtype=BF16),
             vmem(3, SEG, NSEG, 256), vmem(3, 2, NZ * NSEG, LANE),
-            dma((2, 2)), dma((2, 2)),
+            dma((2, 2)), dma((2, 2)), dma(()),
         ],
         compiler_params=pltpu.CompilerParams(vmem_limit_bytes=48 * 2**20),
         cost_estimate=pl.CostEstimate(flops=6 * 10**9, bytes_accessed=20 * 2**20, transcendentals=0),
-    )(e5, s4, tab, down, coz, cox)
-    return (grad_e.reshape(emission.shape), grad_s.reshape(absorption.shape), owned_error)
+    )(e5, s4, tab, coz, cox)
+    return (grad_e.reshape(emission.shape), grad_s.reshape(absorption.shape), owned.reshape(1, 1, 1))
 
 
 def solution(mesh):

time: 162 us -> 66.7 us (0.41)
  blocking collectives: 65.5 us -> 0 us
  Pallas kernels: 85 us -> 57 us
  local copies, waits for them, and re-layouts: 8.12 us -> 6.26 us
    unnamed x1 -> x0, blocking collectives: 65.5 us -> none
    pallas_call x2, Pallas kernels: 85 us -> 57 us  [the longest x1 35.8 us: local(): pl.pallas_call(functools.partial(forward_kernel, 0.25 / step_z, 0.25 / st...]
    unnamed x20 -> x14, local copies, waits for them, and re-layouts: 7.75 us -> 6.26 us
where the time goes in v2:
time: 66.7 us; the launch traced here: 65.8 us
  Pallas kernels  57 us (85%)
  local copies, waits for them, and re-layouts  6.26 us (9%)
  between operations  2.47 us (4%)
    pallas_call x1, Pallas kernels, local(): pl.pallas_call(functools.partial(forward_kernel, 0.25 / step_z, 0.25 / st...  35.8 us
    pallas_call x1, Pallas kernels, local(): pl.pallas_call(functools.partial(backward_kernel, step_z), out_shape=[jax...  21.2 us
    unnamed x14, local copies, waits for them, and re-layouts  6.26 us

profile of v2, /device:TPU:1, one launch (start us, length us, event | category | flops | bytes accessed | tf_op | source)
XLA Modules:
  0.0 65.8 jit_solution(2926631145834001820)
XLA Ops:
  0.6 0.0 copy-start
  0.6 1.6 %copy-done = bf16[32,256,128]{2,1,0:T(8,128)(2,1)S(1)} copy-done((bf16[32,256,128]{2,1,0:T(8,128)(2,1)S(1)}, bf16[32,256,128]{2,1,0:T(8,128)(2,1)}, u32[]{:S(2)}) %copy-start) | copy-done | bytes 2097176
  2.2 0.0 copy-start.1
  2.2 1.4 %copy-done.1 = bf16[3,256,1024]{2,1,0:T(8,128)(2,1)S(1)} copy-done((bf16[3,256,1024]{2,1,0:T(8,128)(2,1)S(1)}, bf16[3,256,1024]{2,1,0:T(8,128)(2,1)}, u32[]{:S(2)}) %copy-start.1) | copy-done | bytes 1572888
  3.6 0.0 copy-start.2
  3.6 0.9 %copy-done.2 = bf16[384,256]{1,0:T(8,128)(2,1)S(1)} copy-done((bf16[384,256]{1,0:T(8,128)(2,1)S(1)}, bf16[384,256]{1,0:T(8,128)(2,1)}, u32[]{:S(2)}) %copy-start.2) | copy-done | bytes 196632
  4.6 0.0 copy-start.4
  4.6 0.9 %copy-done.4 = bf16[256,256]{1,0:T(8,128)(2,1)S(1)} copy-done((bf16[256,256]{1,0:T(8,128)(2,1)S(1)}, bf16[256,256]{1,0:T(8,128)(2,1)}, u32[]{:S(2)}) %copy-start.4) | copy-done | bytes 131096
  5.5 0.0 copy-start.5
  5.5 0.7 %copy-done.5 = s32[4,4,256,1]{2,3,1,0:T(1,128)S(1)} copy-done((s32[4,4,256,1]{2,3,1,0:T(1,128)S(1)}, s32[4,4,256,1]{2,3,1,0:T(1,128)}, u32[]{:S(2)}) %copy-start.5) | copy-done | bytes 16408
  6.2 0.0 copy-start.6
  6.2 0.7 %copy-done.6 = s32[4,8,32,1]{2,3,1,0:T(1,128)S(1)} copy-done((s32[4,8,32,1]{2,3,1,0:T(1,128)S(1)}, s32[4,8,32,1]{2,3,1,0:T(1,128)}, u32[]{:S(2)}) %copy-start.6) | copy-done | bytes 4120
  6.9 0.0 copy-start.3
  6.9 35.8 %shard_map.103 = (f32[32,4,8,256]{3,2,1,0:T(8,128)S(1)}, f32[4,2,256,128]{3,2,1,0:T(8,128)S(1)}, f32[1,1]{1,0:T(1,128)}) custom-call(bf16[3,32,8,32,128]{4,3,2,1,0:T(8,128)(2,1)} %bitcast.11, bf16[32,8,32,128]{3,2,1,0:T(8,128)(2,1)S(1)} %bitcast.7, bf16[3,1024,1024]{2,1,0:T(8,128)(2,1)} %tz_hbm.1, bf16[3,256,1024]{2,1,0:T(8,128)(2,1)S(1)} %copy-done.1, ...), custom_call_target="tpu_custom_call" | custom-call | tf_op jit(solution)/shard_map/pallas_call | solution.py:636
  42.7 0.0 copy-done.3
  42.7 21.2 %shard_map.104 = (bf16[3,32,8,32,128]{4,3,2,1,0:T(8,128)(2,1)}, bf16[32,8,32,128]{3,2,1,0:T(8,128)(2,1)}) custom-call(bf16[3,32,8,32,128]{4,3,2,1,0:T(8,128)(2,1)} %bitcast.12, bf16[32,8,32,128]{3,2,1,0:T(8,128)(2,1)S(1)} %bitcast.8, bf16[384,256]{1,0:T(8,128)(2,1)S(1)} %copy-done.3, f32[32,4,8,256]{3,2,1,0:T(8,128)S(1)} %get-tuple-element.8.coz, ...), custom_call_target="tpu_custom_call" | custom-call | flops 6000000000 | bytes 20971520 | tf_op jit(solution)/shard_map/pallas_call | solution.py:666
Async XLA Ops:
  0.6 1.6 %copy-start = (bf16[32,256,128]{2,1,0:T(8,128)(2,1)S(1)}, bf16[32,256,128]{2,1,0:T(8,128)(2,1)}, u32[]{:S(2)}) copy-start(bf16[32,256,128]{2,1,0:T(8,128)(2,1)} %param.9) | copy-start | bytes 6291460
  2.2 1.4 %copy-start.1 = (bf16[3,256,1024]{2,1,0:T(8,128)(2,1)S(1)}, bf16[3,256,1024]{2,1,0:T(8,128)(2,1)}, u32[]{:S(2)}) copy-start(bf16[3,256,1024]{2,1,0:T(8,128)(2,1)} %tx_hbm.1) | copy-start | bytes 4718596
  3.6 0.9 %copy-start.2 = (bf16[384,256]{1,0:T(8,128)(2,1)S(1)}, bf16[384,256]{1,0:T(8,128)(2,1)}, u32[]{:S(2)}) copy-start(bf16[384,256]{1,0:T(8,128)(2,1)} %constant.4.clone.tab_hbm) | copy-start | bytes 589828
  4.6 0.9 %copy-start.4 = (bf16[256,256]{1,0:T(8,128)(2,1)S(1)}, bf16[256,256]{1,0:T(8,128)(2,1)}, u32[]{:S(2)}) copy-start(bf16[256,256]{1,0:T(8,128)(2,1)} %constant.5.clone.perm_hbm) | copy-start | bytes 393220
  5.5 0.7 %copy-start.5 = (s32[4,4,256,1]{2,3,1,0:T(1,128)S(1)}, s32[4,4,256,1]{2,3,1,0:T(1,128)}, u32[]{:S(2)}) copy-start(s32[4,4,256,1]{2,3,1,0:T(1,128)} %param.12) | copy-start | bytes 49156
  6.2 0.7 %copy-start.6 = (s32[4,8,32,1]{2,3,1,0:T(1,128)S(1)}, s32[4,8,32,1]{2,3,1,0:T(1,128)}, u32[]{:S(2)}) copy-start(s32[4,8,32,1]{2,3,1,0:T(1,128)} %param.13) | copy-start | bytes 12292
  6.9 35.8 %copy-start.3 = (bf16[384,256]{1,0:T(8,128)(2,1)S(1)}, bf16[384,256]{1,0:T(8,128)(2,1)}, u32[]{:S(2)}) copy-start(bf16[384,256]{1,0:T(8,128)(2,1)} %constant.4.clone.tab_hbm) | copy-start | bytes 589828

commit v3 on v2

--- a/solution.py
+++ b/solution.py
@@ -23,6 +23,7 @@
 NZG = NZ // ZG
 STEPS = 2 * NZG
 LANE = 128
+VMEM_LIMIT = 61 * 2**20 + 2**19
 
 
 def interp_table(width):
@@ -43,18 +44,18 @@
             fine[f, z, h, s * PITCH : s * PITCH + HALF] = r[s * HALF : (s + 1) * HALF, half(h)]
 
 
-def upsample_part(ebuf, sbuf, tab, fine, part):
+def upsample_part(ebuf, sbuf, t, tab, fine, part):
     rows = NSEG * HALF
     if part == 0:
-        a = ebuf[0:2].reshape(2 * ZG * rows, LANE)
+        a = ebuf[t, 0:2].reshape(2 * ZG * rows, LANE)
         r = jnp.dot(a, tab[0:LANE], preferred_element_type=F32)
         for f in range(2):
             for z in range(ZG):
                 i = f * ZG + z
                 upsample_store(fine, f, z, r[i * rows : (i + 1) * rows])
     else:
-        r = jnp.dot(ebuf[2].reshape(ZG * rows, LANE), tab[0:LANE], preferred_element_type=F32)
-        s = sbuf[...].reshape(ZG * rows, LANE)
+        r = jnp.dot(ebuf[t, 2].reshape(ZG * rows, LANE), tab[0:LANE], preferred_element_type=F32)
+        s = sbuf[t].reshape(ZG * rows, LANE)
         q = jnp.dot(jnp.concatenate([s, s], axis=1), tab[LANE:], preferred_element_type=F32)
         for z in range(ZG):
             upsample_store(fine, 2, z, r[z * rows : (z + 1) * rows])
@@ -62,57 +63,57 @@
 
 
 class Loader:
-    def __init__(self, e_hbm, s_hbm, ebufs, sbufs, sems):
-        self.refs = (e_hbm, s_hbm, ebufs, sbufs, sems)
-
-    def copies(self, t, b):
-        e_hbm, s_hbm, ebufs, sbufs, sems = self.refs
+    def __init__(self, e_hbm, s_hbm, ebuf, sbuf, sems):
+        self.refs = (e_hbm, s_hbm, ebuf, sbuf, sems)
+
+    def copies(self, t):
+        e_hbm, s_hbm, ebuf, sbuf, sems = self.refs
         k, zg = t // NZG, t % NZG
         zs, xs = pl.ds(zg * ZG, ZG), pl.ds(pl.multiple_of(k * HALF, HALF), HALF)
         return (
-            pltpu.make_async_copy(e_hbm.at[:, zs, :, xs, :], ebufs[b], sems.at[b, 0]),
-            pltpu.make_async_copy(s_hbm.at[zs, :, xs, :], sbufs[b], sems.at[b, 1]),
+            pltpu.make_async_copy(e_hbm.at[:, zs, :, xs, :], ebuf.at[t], sems.at[t, 0]),
+            pltpu.make_async_copy(s_hbm.at[zs, :, xs, :], sbuf.at[t], sems.at[t, 1]),
         )
 
-    def start(self, t, b):
-        for c in self.copies(t, b):
-            c.start()
-
-    def wait(self, t, b):
-        for c in self.copies(t, b):
+    def start(self):
+        def one(t, _):
+            for c in self.copies(t):
+                c.start()
+            return 0
+
+        lax.fori_loop(0, STEPS, one, 0)
+
+    def wait(self, t):
+        for c in self.copies(t):
             c.wait()
 
 
-def forward_scan(fine, zs, zc, xc, k, zg, extra):
+def forward_scan(fine, zc, xc, k, zg, extra):
     for h in range(2):
         hs = half(h)
         rows = [pl.ds(pl.multiple_of((zg * ZG + z) * NSEG, NSEG), NSEG) for z in range(ZG)]
-        carry = [xc[i, h, rows[z], :] for z in range(ZG) for i in range(5)]
+        carry = [[xc[i, h, r, :] for i in range(4)] for r in rows]
         extra(h)
         for xm in range(HALF):
             zr = k * HALF + xm
-            s_z = zs[zr, :, hs]
             c0, c1, c2, t_z = [zc[zr, i, :, hs] for i in range(4)]
             for z in range(ZG):
                 e0, e1, e2, sg = [fine[f, z, h, pl.ds(xm, NSEG, stride=PITCH), :] for f in range(4)]
-                s_z = s_z + sg
-                t_new = jnp.exp2(s_z)
+                t_new = t_z * jnp.exp2(sg)
                 share = t_z - t_new
                 t_z = t_new
                 c0 = c0 + share * e0
                 c1 = c1 + share * e1
                 c2 = c2 + share * e2
-                s_x, t_x, d0, d1, d2 = carry[z * 5 : z * 5 + 5]
-                s_x = s_x + sg
-                t_new = jnp.exp2(s_x * 0.25)
+                d0, d1, d2, t_x = carry[z]
+                t_new = t_x * jnp.exp2(sg * 0.25)
                 share = t_x - t_new
-                carry[z * 5 : z * 5 + 5] = [s_x, t_new, d0 + share * e0, d1 + share * e1, d2 + share * e2]
-            zs[zr, :, hs] = s_z
+                carry[z] = [d0 + share * e0, d1 + share * e1, d2 + share * e2, t_new]
             for i, v in enumerate((c0, c1, c2, t_z)):
                 zc[zr, i, :, hs] = v
         for z in range(ZG):
-            for i in range(5):
-                xc[i, h, rows[z], :] = carry[z * 5 + i]
+            for i in range(4):
+                xc[i, h, rows[z], :] = carry[z][i]
 
 
 def compose(front, back):
@@ -140,21 +141,23 @@
 
 
 def forward_kernel(
-    inv_z, inv_x, share,
+    step_z, step_x, share,
     e_hbm, s_hbm, tz_hbm, tx_hbm, oz_hbm, ox_hbm, tab_hbm, perm_hbm,
-    coz, cox, owned,
-    ebuf0, ebuf1, sbuf0, sbuf1, fine0, fine1, zs, zc, xc,
+    coz_hbm, cox_hbm, owned,
+    ebuf, sbuf, fine0, fine1, zc, xc, coz, cox,
     tzb, txb, tzf, txf,
     sib, pc, got, rep, back, fin, finr,
     xloc, xgot, xrep, xback, xsuf,
     tab, perm, err, ozb, oxb, ez, ex, ey,
-    in_sem, t_sem, sem_sib, sem_chip, sem_rep, sem_fin, sem_x, sem_xr, sem_ez, sem_ex, sem_ey,
+    in_sem, t_sem, sem_sib, sem_chip, sem_rep, sem_fin, sem_x, sem_xr, sem_ez, sem_ex, sem_ey, sem_co,
 ):
     ix, iy, iz = lax.axis_index("gx"), lax.axis_index("gy"), lax.axis_index("gz")
     chip, core = iz // 2, iz % 2
-    load = Loader(e_hbm, s_hbm, (ebuf0, ebuf1), (sbuf0, sbuf1), in_sem)
-    load.start(0, 0)
-    load.start(1, 1)
+    load = Loader(e_hbm, s_hbm, ebuf, sbuf, in_sem)
+    load.start()
+    lane = lax.broadcasted_iota(jnp.int32, (8, LANE), 1)
+    sub = lax.broadcasted_iota(jnp.int32, (8, LANE), 0)
+    weight = jnp.where(lane == 0, 1.0, 0.75)
     px = pl.ds(pl.multiple_of(iy * 256, 256), 256)
     tz_copy = pltpu.make_async_copy(tz_hbm.at[:, pl.ds(pl.multiple_of(ix * 256, 256), 256), px], tzb, t_sem.at[0])
     tx_copy = pltpu.make_async_copy(tx_hbm.at[:, pl.ds(pl.multiple_of(iz * NZ, NZ), NZ), px], txb, t_sem.at[1])
@@ -237,7 +240,7 @@
                 bricks = [[got[k, o, i, f, :, half(h)] for f in range(4)] for o in range(4)]
                 row = k * HALF + core * 8 + m
                 target = [tzf[c, h, pl.ds(row, NSEG, stride=SEG + 4), :] for c in range(3)]
-                replies, s = merge(bricks, target, inv_z)
+                replies, s = merge(bricks, target, weight * (1.0 / step_z))
                 sq = sq + s
                 for o in range(4):
                     for f in range(4):
@@ -259,8 +262,8 @@
                 inner_b = g0 * b[0] + g1 * b[1] + g2 * b[2] + gt * b[3]
                 k_b = -(a[3] * inner_b)
                 k_a = k_b - (g0 * a[0] + g1 * a[1] + g2 * a[2])
-                part_a = (g0, g1, g2, k_a)
-                part_b = (a[3] * g0, a[3] * g1, a[3] * g2, k_b)
+                part_a = (g0, g1, g2, k_a * step_z)
+                part_b = (a[3] * g0, a[3] * g1, a[3] * g2, k_b * step_z)
                 first = core == 0
                 for f in range(4):
                     coz[k * HALF + core * 8 + m, f, :, hs] = jnp.where(first, part_a[f], part_b[f])
@@ -269,10 +272,18 @@
 
         lax.fori_loop(0, 8, body, 0)
         fin_copy(k).start()
+        out_copies(k)[0].start()
+
+    def out_copies(k):
+        mine, other = pl.ds(k * HALF + core * 8, 8), pl.ds(k * HALF + (1 - core) * 8, 8)
+        return (
+            pltpu.make_async_copy(coz.at[mine], coz_hbm.at[mine], sem_co.at[k]),
+            pltpu.make_async_copy(finr.at[k], coz_hbm.at[other], sem_co.at[2 + k]),
+        )
 
     def z_finish(k):
         fin_copy(k).wait_recv()
-        coz[pl.ds(k * HALF + (1 - core) * 8, 8)] = finr[k]
+        out_copies(k)[1].start()
 
     def x_compose():
         for g in range(4):
@@ -280,7 +291,7 @@
                 acc = None
                 for s in range(NSEG):
                     rows = pl.ds(g * 64 + s, 8, stride=NSEG)
-                    seg = tuple(xc[i, h, rows, :] for i in (2, 3, 4, 1))
+                    seg = tuple(xc[i, h, rows, :] for i in range(4))
                     acc = seg if acc is None else compose(acc, seg)
                 for f in range(4):
                     xloc[g, f, :, half(h)] = acc[f]
@@ -295,7 +306,7 @@
         for h in range(2):
             bricks = [[xgot[o, f, :, half(h)] for f in range(4)] for o in range(4)]
             target = [txf[c, pl.ds(pl.multiple_of(ix * 8, 8), 8), half(h)] for c in range(3)]
-            replies, s = merge(bricks, target, inv_x)
+            replies, s = merge(bricks, target, weight * (1.0 / step_x))
             sq = sq + s
             for o in range(4):
                 for f in range(4):
@@ -304,6 +315,8 @@
         for c in xr_copies():
             c.start()
         xback[ix] = xrep[ix]
+
+    cox_copy = pltpu.make_async_copy(cox, cox_hbm, sem_co.at[4])
 
     def x_split():
         for c in xr_copies():
@@ -314,7 +327,7 @@
                 suffix = None
                 for s in reversed(range(NSEG)):
                     rows = pl.ds(g * 64 + s, 8, stride=NSEG)
-                    seg = tuple(xc[i, h, rows, :] for i in (2, 3, 4, 1))
+                    seg = tuple(xc[i, h, rows, :] for i in range(4))
                     suffix = seg if suffix is None else compose(seg, suffix)
                     xsuf[s] = g0 * suffix[0] + g1 * suffix[1] + g2 * suffix[2] + gt * suffix[3]
                 front = jnp.ones((8, LANE), F32)
@@ -323,11 +336,9 @@
                     cox[0, h, rows, :] = front * g0
                     cox[1, h, rows, :] = front * g1
                     cox[2, h, rows, :] = front * g2
-                    cox[3, h, rows, :] = -(front * xsuf[s])
-                    front = front * xc[1, h, rows, :]
-
-    lane = lax.broadcasted_iota(jnp.int32, (8, LANE), 1)
-    sub = lax.broadcasted_iota(jnp.int32, (8, LANE), 0)
+                    cox[3, h, rows, :] = front * xsuf[s] * (-step_x)
+                    front = front * xc[3, h, rows, :]
+        cox_copy.start()
 
     def scatter(sq, ids):
         owner = jnp.zeros((8, LANE), jnp.int32)
@@ -374,11 +385,9 @@
         mine = jnp.where(lane == ix * 32 + iy * 8 + iz, total, 0.0)
         owned[0, 0] = jnp.sum(mine) * share
 
-    zs[...] = jnp.zeros_like(zs)
-    xc[0] = jnp.zeros_like(xc[0])
-    xc[1] = jnp.ones_like(xc[1])
-    for i in (2, 3, 4):
+    for i in range(3):
         xc[i] = jnp.zeros_like(xc[i])
+    xc[3] = jnp.ones_like(xc[3])
 
     def clear(m, _):
         for f in range(4):
@@ -386,30 +395,23 @@
         return 0
 
     lax.fori_loop(0, SEG, clear, 0)
-    load.wait(0, 0)
     tab_copy.wait()
+    load.wait(0)
     for part in range(2):
-        upsample_part(ebuf0, sbuf0, tab, fine0, part)
-
-    bufs = ((ebuf0, sbuf0, fine0), (ebuf1, sbuf1, fine1))
+        upsample_part(ebuf, sbuf, 0, tab, fine0, part)
 
     def pair_of_steps(i, _):
-        for b in range(2):
-            t = i * 2 + b
-            k, zg = t // NZG, t % NZG
-            other = bufs[1 - b]
-
-            @pl.when(t + 2 < STEPS)
-            def _():
-                load.start(t + 2, b)
-
-            @pl.when(t + 1 < STEPS)
-            def _():
-                load.wait(t + 1, 1 - b)
-
+        t = i * 2
+        load.wait(t + 1)
+
+        @pl.when(t + 2 < STEPS)
+        def _():
+            load.wait(t + 2)
+
+        for b, (fine, ahead) in enumerate(((fine0, fine1), (fine1, fine0))):
             forward_scan(
-                bufs[b][2], zs, zc, xc, k, zg,
-                lambda part: upsample_part(other[0], other[1], tab, other[2], part),
+                fine, zc, xc, t // NZG, t % NZG + b,
+                lambda part: upsample_part(ebuf, sbuf, t + b + 1, tab, ahead, part),
             )
 
         @pl.when(i == 3)
@@ -455,149 +457,152 @@
             c.wait_send()
     for c in x_copies() + xr_copies() + ez_copies() + ex_copies() + ey_copies():
         c.wait_send()
-
-
-def project_down(even, odd, first, last, near, far):
-    side = jnp.where(first, even, pltpu.roll(odd, 1, axis=1)) + jnp.where(last, odd, pltpu.roll(even, LANE - 1, axis=1))
-    return near * (even + odd) + (side if far is None else far * side)
-
-
-def backward_scan(fine, zcar, xcar, coz, cox, coarse, k, zg, pair, far):
-    lanes = lax.broadcasted_iota(jnp.int32, (NSEG, LANE), 1)
-    first, last = lanes == 0, lanes == LANE - 1
+    for c in out_copies(0) + out_copies(1) + (cox_copy,):
+        c.wait()
+
+
+def project_down(even, odd, third):
+    return even + third * odd + pltpu.roll(odd + third * even, LANE - 1, axis=1)
+
+
+def backward_scan(fine, zcar, xcar, coz, cox, coarse, k, zg, pair, third):
     planes = [pair * 2 + i for i in range(2)]
     rows = [pl.ds(pl.multiple_of((zg * ZG + z) * NSEG, NSEG), NSEG) for z in planes]
-    carry = [[[xcar[i, h, r, :] for i in range(3)] for h in range(2)] for r in rows]
+    carry = [[[xcar[i, h, r, :] for i in range(2)] for h in range(2)] for r in rows]
     gx = [[[cox[c, h, r, :] for c in range(3)] for h in range(2)] for r in rows]
     for xm in range(HALF):
         zr = k * HALF + xm
-        z_carry = [[zcar[i, zr, :, half(h)] for i in range(3)] for h in range(2)]
+        z_carry = [[zcar[i, zr, :, half(h)] for i in range(2)] for h in range(2)]
         gz = [[coz[zr, c, :, half(h)] for c in range(3)] for h in range(2)]
         for n, z in enumerate(planes):
             out = [[None] * 2 for _ in range(4)]
             for h in range(2):
                 e0, e1, e2, sg = [fine[f, z, h, pl.ds(xm, NSEG, stride=PITCH), :] for f in range(4)]
                 g0, g1, g2 = gz[h]
-                s_z, t_z, a_z = z_carry[h]
-                s_z = s_z + sg
-                t_new = jnp.exp2(s_z)
+                t_z, a_z = z_carry[h]
+                t_new = t_z * jnp.exp2(sg)
                 share_z = t_z - t_new
                 inner = g0 * e0 + g1 * e1 + g2 * e2
                 a_z = a_z + share_z * inner
                 grad = t_new * inner + a_z
-                z_carry[h] = [s_z, t_new, a_z]
+                z_carry[h] = [t_new, a_z]
                 h0, h1, h2 = gx[n][h]
-                s_x, t_x, a_x = carry[n][h]
-                s_x = s_x + sg
-                t_new = jnp.exp2(s_x * 0.25)
+                t_x, a_x = carry[n][h]
+                t_new = t_x * jnp.exp2(sg * 0.25)
                 share_x = t_x - t_new
-                inner = h0 * e0 + h1 * e1 + h2 * e2
+                q0, q1, q2 = [cox[4 + c, h, rows[n], :] for c in range(3)]
+                inner = q0 * e0 + q1 * e1 + q2 * e2
                 a_x = a_x + share_x * inner
-                out[3][h] = grad + 0.25 * (t_new * inner + a_x)
-                carry[n][h] = [s_x, t_new, a_x]
+                out[3][h] = (grad + a_x) + t_new * inner
+                carry[n][h] = [t_new, a_x]
                 out[0][h] = g0 * share_z + h0 * share_x
                 out[1][h] = g1 * share_z + h1 * share_x
                 out[2][h] = g2 * share_z + h2 * share_x
             for f in range(4):
-                v = project_down(out[f][0], out[f][1], first, last, 3.0 * far if f == 3 else 3.0, far if f == 3 else None)
-                coarse[f, z, pl.ds(xm, NSEG, stride=PITCH), :] = v
+                coarse[f, z, pl.ds(xm, NSEG, stride=PITCH), :] = project_down(out[f][0], out[f][1], third)
         for h in range(2):
-            for i in range(3):
+            for i in range(2):
                 zcar[i, zr, :, half(h)] = z_carry[h][i]
     for n, r in enumerate(rows):
         for h in range(2):
-            for i in range(3):
+            for i in range(2):
                 xcar[i, h, r, :] = carry[n][h][i]
 
 
-def narrow_part(coarse, eout, sout, part):
+def narrow_part(coarse, eout, sout, t, part):
     for z in (2 * part, 2 * part + 1):
         for f in range(4):
             for s in range(NSEG):
                 v = coarse[f, z, pl.ds(s * PITCH, HALF), :].astype(BF16)
                 if f == 3:
-                    sout[z, s] = v
+                    sout[t, z, s] = v
                 else:
-                    eout[f, z, s] = v
+                    eout[t, f, z, s] = v
 
 
 def backward_kernel(
-    far,
-    e_hbm, s_hbm, tab_hbm, coz, cox,
+    e_hbm, s_hbm, tab_hbm, coz_hbm, cox_hbm,
     ge_hbm, gs_hbm,
-    ebuf0, ebuf1, sbuf0, sbuf1, fine0, fine1, tab, coarse0, coarse1,
-    eout0, eout1, sout0, sout1, zcar, xcar,
-    in_sem, out_sem, tab_sem,
+    ebuf, sbuf, fine0, fine1, tab, coarse0, coarse1,
+    eout, sout, zcar, xcar, coz, cox,
+    in_sem, out_sem, co_sem,
 ):
-    tab_copy = pltpu.make_async_copy(tab_hbm, tab, tab_sem)
+    tab_copy = pltpu.make_async_copy(tab_hbm, tab, co_sem.at[0])
+    coz_copy = pltpu.make_async_copy(coz_hbm, coz, co_sem.at[1])
+    cox_copy = pltpu.make_async_copy(cox_hbm, cox.at[pl.ds(0, 4)], co_sem.at[2])
     tab_copy.start()
-    load = Loader(e_hbm, s_hbm, (ebuf0, ebuf1), (sbuf0, sbuf1), in_sem)
-    load.start(0, 0)
-    load.start(1, 1)
-    eouts, souts = (eout0, eout1), (sout0, sout1)
-
-    def stores(t, b):
+    load = Loader(e_hbm, s_hbm, ebuf, sbuf, in_sem)
+    for c in load.copies(0):
+        c.start()
+    coz_copy.start()
+    cox_copy.start()
+
+    def rest(t, _):
+        for c in load.copies(t):
+            c.start()
+        return 0
+
+    lax.fori_loop(1, STEPS, rest, 0)
+
+    def stores(t):
         k, zg = t // NZG, t % NZG
         zr, xr = pl.ds(zg * ZG, ZG), pl.ds(pl.multiple_of(k * HALF, HALF), HALF)
         return (
-            pltpu.make_async_copy(eouts[b], ge_hbm.at[:, zr, :, xr, :], out_sem.at[b, 0]),
-            pltpu.make_async_copy(souts[b], gs_hbm.at[zr, :, xr, :], out_sem.at[b, 1]),
+            pltpu.make_async_copy(eout.at[t], ge_hbm.at[:, zr, :, xr, :], out_sem.at[t, 0]),
+            pltpu.make_async_copy(sout.at[t], gs_hbm.at[zr, :, xr, :], out_sem.at[t, 1]),
         )
 
-    zcar[0] = jnp.zeros_like(zcar[0])
-    zcar[1] = jnp.ones_like(zcar[1])
-    zcar[2] = coz[:, 3]
-    xcar[0] = jnp.zeros_like(xcar[0])
-    xcar[1] = jnp.ones_like(xcar[1])
-    xcar[2] = cox[3]
-    load.wait(0, 0)
+    def store(t):
+        for c in stores(t):
+            c.start()
+
+    zcar[0] = jnp.ones_like(zcar[0])
+    xcar[0] = jnp.ones_like(xcar[0])
+    third = jnp.where(lax.broadcasted_iota(jnp.int32, (NSEG, LANE), 1) == 0, 0.0, 1.0 / 3.0)
     tab_copy.wait()
+    load.wait(0)
     for part in range(2):
-        upsample_part(ebuf0, sbuf0, tab, fine0, part)
-    bufs = ((ebuf0, sbuf0, fine0, coarse0), (ebuf1, sbuf1, fine1, coarse1))
+        upsample_part(ebuf, sbuf, 0, tab, fine0, part)
+    coz_copy.wait()
+    cox_copy.wait()
+    zcar[1] = coz[:, 3]
+    xcar[1] = cox[3]
+    for c in range(3):
+        cox[4 + c] = 0.25 * cox[c]
 
     def pair_of_steps(i, _):
-        for b in range(2):
-            t = i * 2 + b
-            k, zg = t // NZG, t % NZG
-            other = bufs[1 - b]
-
-            @pl.when(t + 2 < STEPS)
-            def _():
-                load.start(t + 2, b)
-
-            @pl.when(t + 1 < STEPS)
-            def _():
-                load.wait(t + 1, 1 - b)
-
-            @pl.when(t >= 3)
-            def _():
-                for c in stores(t - 3, 1 - b):
-                    c.wait()
-
+        t = i * 2
+        load.wait(t + 1)
+
+        @pl.when(t + 2 < STEPS)
+        def _():
+            load.wait(t + 2)
+
+        for b, (fine, ahead, new, old) in enumerate(((fine0, fine1, coarse0, coarse1), (fine1, fine0, coarse1, coarse0))):
+            before = lax.rem(t + b + STEPS, STEPS + 1)
             for part in range(2):
-                upsample_part(other[0], other[1], tab, other[2], part)
-                narrow_part(other[3], eouts[1 - b], souts[1 - b], part)
-                backward_scan(bufs[b][2], zcar, xcar, coz, cox, bufs[b][3], k, zg, part, far)
-
-            @pl.when(t >= 1)
-            def _():
-                for c in stores(t - 1, 1 - b):
-                    c.start()
-
+                upsample_part(ebuf, sbuf, t + b + 1, tab, ahead, part)
+                narrow_part(old, eout, sout, before, part)
+                backward_scan(fine, zcar, xcar, coz, cox, new, t // NZG, t % NZG + b, part, third)
+
+        @pl.when(i > 0)
+        def _():
+            store(t - 1)
+
+        store(t)
         return 0
 
     lax.fori_loop(0, STEPS // 2, pair_of_steps, 0)
-    last = (STEPS - 1) % 2
-    for c in stores(STEPS - 3, last):
-        c.wait()
     for part in range(2):
-        narrow_part(bufs[last][3], eouts[last], souts[last], part)
-    for c in stores(STEPS - 1, last):
-        c.start()
-    for t in (STEPS - 2, STEPS - 1):
-        for c in stores(t, t % 2):
+        narrow_part(coarse1, eout, sout, STEPS - 1, part)
+    store(STEPS - 1)
+
+    def finish(t, _):
+        for c in stores(t):
             c.wait()
+        return 0
+
+    lax.fori_loop(0, STEPS, finish, 0)
 
 
 def vmem(*shape, dtype=F32):
@@ -605,7 +610,6 @@
 
 
 HBM = pl.BlockSpec(memory_space=pltpu.HBM)
-IN_VMEM = pl.BlockSpec(memory_space=pltpu.VMEM)
 
 
 def local(emission, absorption, target_z, target_x, owner_z, owner_x):
@@ -618,32 +622,32 @@
     step_x = OPTICAL / (width_x * count_x)
     interp = interp_table(width_y)
     rate = interp.T * (-step_z * math.log2(math.e))
-    order = np.concatenate([np.arange(0, pixels, 2), np.arange(1, pixels, 2)])
+    order = np.concatenate([np.arange(0, pixels, 2), np.roll(np.arange(1, pixels, 2), 1)])
     rate_hi = rate.astype(BF16)
     rate_lo = (rate - rate_hi.astype(np.float64)).astype(BF16)
     tab = np.concatenate([interp.T.astype(BF16), rate_hi, rate_lo], axis=0)[:, order]
+    tab_back = np.concatenate([(interp.T * step_z).astype(BF16), rate_hi, rate_lo], axis=0)[:, order]
     perm = np.eye(pixels)[:, order].astype(BF16)
     slots = 2 * width_x // (count_y * count_z) + 2 * depth_z // (count_x * count_y)
     e5 = emission.reshape(3, depth_z, NSEG, SEG, width_y)
     s4 = absorption.reshape(depth_z, NSEG, SEG, width_y)
 
     buffers = [
-        vmem(3, ZG, NSEG, HALF, LANE, dtype=BF16), vmem(3, ZG, NSEG, HALF, LANE, dtype=BF16),
-        vmem(ZG, NSEG, HALF, LANE, dtype=BF16), vmem(ZG, NSEG, HALF, LANE, dtype=BF16),
+        vmem(STEPS + 1, 3, ZG, NSEG, HALF, LANE, dtype=BF16), vmem(STEPS + 1, ZG, NSEG, HALF, LANE, dtype=BF16),
         vmem(4, ZG, 2, NSEG * PITCH, LANE), vmem(4, ZG, 2, NSEG * PITCH, LANE),
     ]
     dma = pltpu.SemaphoreType.DMA
     coz, cox, owned = pl.pallas_call(
-        functools.partial(forward_kernel, 0.25 / step_z, 0.25 / step_x, 1.0 / (3.0 * pixels * slots)),
+        functools.partial(forward_kernel, step_z, step_x, 1.0 / (3.0 * pixels * slots)),
         out_shape=[
             jax.ShapeDtypeStruct((SEG, 4, NSEG, 256), F32),
             jax.ShapeDtypeStruct((4, 2, NZ * NSEG, LANE), F32),
             jax.ShapeDtypeStruct((1, 1), F32),
         ],
         in_specs=[HBM] * 8,
-        out_specs=[IN_VMEM, IN_VMEM, pl.BlockSpec(memory_space=pltpu.SMEM)],
+        out_specs=[HBM, HBM, pl.BlockSpec(memory_space=pltpu.SMEM)],
         scratch_shapes=buffers + [
-            vmem(SEG, NSEG, 256), vmem(SEG, 4, NSEG, 256), vmem(5, 2, NZ * NSEG, LANE),
+            vmem(SEG, 4, NSEG, 256), vmem(4, 2, NZ * NSEG, LANE), vmem(SEG, 4, NSEG, 256), vmem(4, 2, NZ * NSEG, LANE),
             vmem(3, 256, 256, dtype=BF16), vmem(3, NZ, 256, dtype=BF16),
             vmem(3, 2, NSEG * (SEG + 4), LANE), vmem(3, NZ, 256),
             vmem(2, 8, 4, 8, 256), vmem(2, 8, 4, 8, 256), vmem(2, 4, 2, 4, 8, 256), vmem(2, 4, 2, 4, 8, 256),
@@ -652,11 +656,11 @@
             vmem(3 * LANE, 256, dtype=BF16), vmem(256, 256, dtype=BF16), vmem(5, 8, LANE),
             pltpu.SMEM((1, 256), jnp.int32), pltpu.SMEM((1, NZ), jnp.int32),
             vmem(8, 8, LANE), vmem(4, 8, LANE), vmem(4, 8, LANE),
-            dma((2, 2)), dma((6,)), dma((2, 2)), dma((2, 3, 2)), dma((2, 3, 2)), dma((2, 2)), dma((3, 2)), dma((3, 2)),
-            dma((7, 2)), dma((3, 2)), dma((3, 2)),
+            dma((STEPS, 2)), dma((6,)), dma((2, 2)), dma((2, 3, 2)), dma((2, 3, 2)), dma((2, 2)), dma((3, 2)), dma((3, 2)),
+            dma((7, 2)), dma((3, 2)), dma((3, 2)), dma((5,)),
         ],
         compiler_params=pltpu.CompilerParams(
-            collective_id=0, has_side_effects=True, vmem_limit_bytes=48 * 2**20
+            collective_id=0, has_side_effects=True, vmem_limit_bytes=VMEM_LIMIT
         ),
     )(
         e5, s4, target_z, target_x, owner_z.reshape(count_x, count_y, 1, width_x),
@@ -664,20 +668,19 @@
     )
 
     grad_e, grad_s = pl.pallas_call(
-        functools.partial(backward_kernel, step_z),
+        backward_kernel,
         out_shape=[jax.ShapeDtypeStruct(e5.shape, BF16), jax.ShapeDtypeStruct(s4.shape, BF16)],
-        in_specs=[HBM, HBM, HBM, IN_VMEM, IN_VMEM],
+        in_specs=[HBM] * 5,
         out_specs=[HBM, HBM],
         scratch_shapes=buffers + [
             vmem(3 * LANE, 256, dtype=BF16), vmem(4, ZG, NSEG * PITCH, LANE), vmem(4, ZG, NSEG * PITCH, LANE),
-            vmem(3, ZG, NSEG, HALF, LANE, dtype=BF16), vmem(3, ZG, NSEG, HALF, LANE, dtype=BF16),
-            vmem(ZG, NSEG, HALF, LANE, dtype=BF16), vmem(ZG, NSEG, HALF, LANE, dtype=BF16),
-            vmem(3, SEG, NSEG, 256), vmem(3, 2, NZ * NSEG, LANE),
-            dma((2, 2)), dma((2, 2)), dma(()),
+            vmem(STEPS + 1, 3, ZG, NSEG, HALF, LANE, dtype=BF16), vmem(STEPS + 1, ZG, NSEG, HALF, LANE, dtype=BF16),
+            vmem(2, SEG, NSEG, 256), vmem(2, 2, NZ * NSEG, LANE), vmem(SEG, 4, NSEG, 256), vmem(7, 2, NZ * NSEG, LANE),
+            dma((STEPS, 2)), dma((STEPS, 2)), dma((3,)),
         ],
-        compiler_params=pltpu.CompilerParams(vmem_limit_bytes=48 * 2**20),
+        compiler_params=pltpu.CompilerParams(vmem_limit_bytes=VMEM_LIMIT),
         cost_estimate=pl.CostEstimate(flops=6 * 10**9, bytes_accessed=20 * 2**20, transcendentals=0),
-    )(e5, s4, tab, coz, cox)
+    )(e5, s4, tab_back, coz, cox)
     return (grad_e.reshape(emission.shape), grad_s.reshape(absorption.shape), owned.reshape(1, 1, 1))
 
 

time: 66.7 us -> 61.2 us (0.918); the launches traced: 65.8 us -> 61.1 us
  local copies, waits for them, and re-layouts: 6.26 us -> 0 us
  Pallas kernels: 57 us -> 58.7 us
    unnamed x14 -> x0, local copies, waits for them, and re-layouts: 6.26 us -> none
    pallas_call x2, Pallas kernels: 57 us -> 58.7 us  [the longest x1 38.1 us: local(): pl.pallas_call(functools.partial(forward_kernel, step_z, step_x, 1.0 / (3...]
where the time goes in v3:
time: 61.2 us; the launch traced here: 61.1 us
  Pallas kernels  58.7 us (96%)
  between operations  2.39 us (4%)
    pallas_call x1, Pallas kernels, local(): pl.pallas_call(functools.partial(forward_kernel, step_z, step_x, 1.0 / (3...  38.1 us
    pallas_call x1, Pallas kernels, local(): pl.pallas_call(backward_kernel, out_shape=[jax.ShapeDtypeStruct(e5.shape,...  20.6 us

profile of v3, /device:TPU:1, one launch (start us, length us, event | category | flops | bytes accessed | tf_op | source)
XLA Modules:
  0.0 61.1 jit_solution(4025605998514716285)
XLA Ops:
  0.6 38.1 %shard_map.112 = (f32[32,4,8,256]{3,2,1,0:T(8,128)}, f32[4,2,256,128]{3,2,1,0:T(8,128)}, f32[1,1]{1,0:T(1,128)}) custom-call(bf16[3,32,8,32,128]{4,3,2,1,0:T(8,128)(2,1)} %bitcast.7, bf16[32,8,32,128]{3,2,1,0:T(8,128)(2,1)} %bitcast.9, bf16[3,1024,1024]{2,1,0:T(8,128)(2,1)} %tz_hbm.1, bf16[3,256,1024]{2,1,0:T(8,128)(2,1)} %tx_hbm.1, ...), custom_call_target="tpu_custom_call" | custom-call | tf_op jit(solution)/shard_map/pallas_call | solution.py:640
  38.8 20.6 %shard_map.113 = (bf16[3,32,8,32,128]{4,3,2,1,0:T(8,128)(2,1)}, bf16[32,8,32,128]{3,2,1,0:T(8,128)(2,1)}) custom-call(bf16[3,32,8,32,128]{4,3,2,1,0:T(8,128)(2,1)} %bitcast.8, bf16[32,8,32,128]{3,2,1,0:T(8,128)(2,1)} %bitcast.10, bf16[384,256]{1,0:T(8,128)(2,1)} %constant.8.clone.tab_hbm, f32[32,4,8,256]{3,2,1,0:T(8,128)} %get-tuple-element.8.coz_hbm, ...), custom_call_target="tpu_custom_call" | custom-call | flops 6000000000 | bytes 20971520 | tf_op jit(solution)/shard_map/pallas_call | solution.py:670

commit v4 on v3

--- a/solution.py
+++ b/solution.py
@@ -63,25 +63,26 @@
 
 
 class Loader:
-    def __init__(self, e_hbm, s_hbm, ebuf, sbuf, sems):
+    def __init__(self, e_hbm, s_hbm, ebuf, sbuf, sems, base):
         self.refs = (e_hbm, s_hbm, ebuf, sbuf, sems)
+        self.base = base
 
     def copies(self, t):
         e_hbm, s_hbm, ebuf, sbuf, sems = self.refs
-        k, zg = t // NZG, t % NZG
+        k, zg = (self.base + t) // NZG, (self.base + t) % NZG
         zs, xs = pl.ds(zg * ZG, ZG), pl.ds(pl.multiple_of(k * HALF, HALF), HALF)
         return (
             pltpu.make_async_copy(e_hbm.at[:, zs, :, xs, :], ebuf.at[t], sems.at[t, 0]),
             pltpu.make_async_copy(s_hbm.at[zs, :, xs, :], sbuf.at[t], sems.at[t, 1]),
         )
 
-    def start(self):
+    def start(self, first, end):
         def one(t, _):
             for c in self.copies(t):
                 c.start()
             return 0
 
-        lax.fori_loop(0, STEPS, one, 0)
+        lax.fori_loop(first, end, one, 0)
 
     def wait(self, t):
         for c in self.copies(t):
@@ -142,19 +143,20 @@
 
 def forward_kernel(
     step_z, step_x, share,
-    e_hbm, s_hbm, tz_hbm, tx_hbm, oz_hbm, ox_hbm, tab_hbm, perm_hbm,
-    coz_hbm, cox_hbm, owned,
+    e_hbm, s_hbm, tz_hbm, tx_hbm, oz_hbm, ox_hbm, tab_hbm, perm_hbm, back_hbm,
+    coz_hbm, cox_hbm, xst_hbm, ge0_hbm, gs0_hbm, owned,
     ebuf, sbuf, fine0, fine1, zc, xc, coz, cox,
+    tab_back, coarse0, coarse1, eout, sout, zcar, xcar,
     tzb, txb, tzf, txf,
     sib, pc, got, rep, back, fin, finr,
     xloc, xgot, xrep, xback, xsuf,
     tab, perm, err, ozb, oxb, ez, ex, ey,
-    in_sem, t_sem, sem_sib, sem_chip, sem_rep, sem_fin, sem_x, sem_xr, sem_ez, sem_ex, sem_ey, sem_co,
+    in_sem, t_sem, sem_sib, sem_chip, sem_rep, sem_fin, sem_x, sem_xr, sem_ez, sem_ex, sem_ey, sem_co, sem_out, sem_xst,
 ):
     ix, iy, iz = lax.axis_index("gx"), lax.axis_index("gy"), lax.axis_index("gz")
     chip, core = iz // 2, iz % 2
-    load = Loader(e_hbm, s_hbm, ebuf, sbuf, in_sem)
-    load.start()
+    load = Loader(e_hbm, s_hbm, ebuf, sbuf, in_sem, 0)
+    load.start(0, STEPS)
     lane = lax.broadcasted_iota(jnp.int32, (8, LANE), 1)
     sub = lax.broadcasted_iota(jnp.int32, (8, LANE), 0)
     weight = jnp.where(lane == 0, 1.0, 0.75)
@@ -165,8 +167,9 @@
     ox_copy = pltpu.make_async_copy(ox_hbm.at[iy, iz], oxb, t_sem.at[3])
     tab_copy = pltpu.make_async_copy(tab_hbm, tab, t_sem.at[4])
     perm_copy = pltpu.make_async_copy(perm_hbm, perm, t_sem.at[5])
+    back_copy = pltpu.make_async_copy(back_hbm, tab_back, t_sem.at[6])
     tab_copy.start()
-    late = (tz_copy, tx_copy, oz_copy, ox_copy, perm_copy)
+    late = (tz_copy, tx_copy, oz_copy, ox_copy, perm_copy, back_copy)
     for c in late:
         c.start()
 
@@ -266,24 +269,16 @@
                 part_b = (a[3] * g0, a[3] * g1, a[3] * g2, k_b * step_z)
                 first = core == 0
                 for f in range(4):
-                    coz[k * HALF + core * 8 + m, f, :, hs] = jnp.where(first, part_a[f], part_b[f])
+                    coz[k, core * 8 + m, f, :, hs] = jnp.where(first, part_a[f], part_b[f])
                     fin[k, m, f, :, hs] = jnp.where(first, part_b[f], part_a[f])
             return 0
 
         lax.fori_loop(0, 8, body, 0)
         fin_copy(k).start()
-        out_copies(k)[0].start()
-
-    def out_copies(k):
-        mine, other = pl.ds(k * HALF + core * 8, 8), pl.ds(k * HALF + (1 - core) * 8, 8)
-        return (
-            pltpu.make_async_copy(coz.at[mine], coz_hbm.at[mine], sem_co.at[k]),
-            pltpu.make_async_copy(finr.at[k], coz_hbm.at[other], sem_co.at[2 + k]),
-        )
-
-    def z_finish(k):
-        fin_copy(k).wait_recv()
-        out_copies(k)[1].start()
+
+    mine, other = pl.ds(core * 8, 8), pl.ds((1 - core) * 8, 8)
+    mine_copy = pltpu.make_async_copy(coz.at[1, mine], coz_hbm.at[mine], sem_co.at[0])
+    other_copy = pltpu.make_async_copy(finr.at[1], coz_hbm.at[other], sem_co.at[1])
 
     def x_compose():
         for g in range(4):
@@ -316,7 +311,7 @@
             c.start()
         xback[ix] = xrep[ix]
 
-    cox_copy = pltpu.make_async_copy(cox, cox_hbm, sem_co.at[4])
+    cox_copy = pltpu.make_async_copy(cox, cox_hbm, sem_co.at[2])
 
     def x_split():
         for c in xr_copies():
@@ -337,6 +332,8 @@
                     cox[1, h, rows, :] = front * g1
                     cox[2, h, rows, :] = front * g2
                     cox[3, h, rows, :] = front * xsuf[s] * (-step_x)
+                    for c in range(3):
+                        cox[4 + c, h, rows, :] = 0.25 * cox[c, h, rows, :]
                     front = front * xc[3, h, rows, :]
         cox_copy.start()
 
@@ -401,17 +398,16 @@
         upsample_part(ebuf, sbuf, 0, tab, fine0, part)
 
     def pair_of_steps(i, _):
-        t = i * 2
-        load.wait(t + 1)
-
-        @pl.when(t + 2 < STEPS)
-        def _():
-            load.wait(t + 2)
-
         for b, (fine, ahead) in enumerate(((fine0, fine1), (fine1, fine0))):
+            t = i * 2 + b
+
+            @pl.when(t + 1 < STEPS)
+            def _():
+                load.wait(t + 1)
+
             forward_scan(
-                fine, zc, xc, t // NZG, t % NZG + b,
-                lambda part: upsample_part(ebuf, sbuf, t + b + 1, tab, ahead, part),
+                fine, zc, xc, t // NZG, t % NZG,
+                lambda part: upsample_part(ebuf, sbuf, t + 1, tab, ahead, part),
             )
 
         @pl.when(i == 3)
@@ -442,38 +438,77 @@
     lax.fori_loop(0, 3, widen, 0)
     z_merge(0)
     z_compose(1)
+    for part in range(2):
+        upsample_part(ebuf, sbuf, 0, tab_back, fine0, part)
+    zcar[0] = jnp.ones_like(zcar[0])
+    xcar[0] = jnp.ones_like(xcar[0])
     x_merge()
     z_split(0)
     z_merge(1)
     err_start()
     x_split()
-    z_finish(0)
-    z_split(1)
-    err_middle()
-    z_finish(1)
+    xcar[1] = cox[3]
+    fin_copy(0).wait_recv()
+    coz[0, other] = finr[0]
+    zcar[1] = coz[0, :, 3]
+
+    def stores(t):
+        return store_copies(eout, sout, ge0_hbm, gs0_hbm, sem_out, t)
+
+    def store(t):
+        for c in stores(t):
+            c.start()
+
+    def state_copy(i):
+        rows = pl.ds(pl.multiple_of(i * 2 * ZG * NSEG, 2 * ZG * NSEG), 2 * ZG * NSEG)
+        return pltpu.make_async_copy(xcar.at[:, :, rows, :], xst_hbm.at[:, :, rows, :], sem_xst.at[i])
+
+    def after(i):
+        state_copy(i).start()
+
+        @pl.when(i == 1)
+        def _():
+            z_split(1)
+            mine_copy.start()
+            err_middle()
+
+    backward_steps(
+        lambda t: None, after, store, ebuf, sbuf, tab_back, (fine0, fine1), (coarse0, coarse1),
+        eout, sout, zcar, xcar, coz.at[0], cox,
+    )
+    fin_copy(1).wait_recv()
+    other_copy.start()
     err_finish()
     for k in range(2):
         for c in [sib_copy(k)] + chip_copies(k) + rep_copies(k) + [fin_copy(k)]:
             c.wait_send()
     for c in x_copies() + xr_copies() + ez_copies() + ex_copies() + ey_copies():
         c.wait_send()
-    for c in out_copies(0) + out_copies(1) + (cox_copy,):
+    for c in (mine_copy, other_copy, cox_copy):
         c.wait()
+
+    def finish(t, _):
+        for c in stores(t):
+            c.wait()
+        return 0
+
+    lax.fori_loop(0, NZG, finish, 0)
+    for i in range(NZG // 2):
+        state_copy(i).wait()
 
 
 def project_down(even, odd, third):
     return even + third * odd + pltpu.roll(odd + third * even, LANE - 1, axis=1)
 
 
-def backward_scan(fine, zcar, xcar, coz, cox, coarse, k, zg, pair, third):
+def backward_scan(fine, zcar, xcar, coz, cox, coarse, zg, pair, third):
     planes = [pair * 2 + i for i in range(2)]
     rows = [pl.ds(pl.multiple_of((zg * ZG + z) * NSEG, NSEG), NSEG) for z in planes]
     carry = [[[xcar[i, h, r, :] for i in range(2)] for h in range(2)] for r in rows]
     gx = [[[cox[c, h, r, :] for c in range(3)] for h in range(2)] for r in rows]
     for xm in range(HALF):
-        zr = k * HALF + xm
-        z_carry = [[zcar[i, zr, :, half(h)] for i in range(2)] for h in range(2)]
-        gz = [[coz[zr, c, :, half(h)] for c in range(3)] for h in range(2)]
+        z_carry = [[zcar[i, xm, :, half(h)] for i in range(2)] for h in range(2)]
+        gz = [[coz[xm, c, :, half(h)] for c in range(3)] for h in range(2)]
         for n, z in enumerate(planes):
             out = [[None] * 2 for _ in range(4)]
             for h in range(2):
@@ -502,7 +537,7 @@
                 coarse[f, z, pl.ds(xm, NSEG, stride=PITCH), :] = project_down(out[f][0], out[f][1], third)
         for h in range(2):
             for i in range(2):
-                zcar[i, zr, :, half(h)] = z_carry[h][i]
+                zcar[i, xm, :, half(h)] = z_carry[h][i]
     for n, r in enumerate(rows):
         for h in range(2):
             for i in range(2):
@@ -520,89 +555,104 @@
                     eout[t, f, z, s] = v
 
 
+def lane_third():
+    return jnp.where(lax.broadcasted_iota(jnp.int32, (NSEG, LANE), 1) == 0, 0.0, 1.0 / 3.0)
+
+
+def backward_steps(ahead_wait, after, store, ebuf, sbuf, tab, fines, coarses, eout, sout, zcar, xcar, coz, cox):
+    third = lane_third()
+    fine0, fine1 = fines
+    coarse0, coarse1 = coarses
+
+    def pair_of_steps(i, _):
+        for b, (fine, ahead, new, old) in enumerate(((fine0, fine1, coarse0, coarse1), (fine1, fine0, coarse1, coarse0))):
+            t = i * 2 + b
+            ahead_wait(t + 1)
+            for part in range(2):
+                upsample_part(ebuf, sbuf, t + 1, tab, ahead, part)
+                narrow_part(old, eout, sout, lax.rem(t + NZG, NZG + 1), part)
+                backward_scan(fine, zcar, xcar, coz, cox, new, t, part, third)
+
+            @pl.when(t > 0)
+            def _():
+                store(t - 1)
+
+        after(i)
+        return 0
+
+    lax.fori_loop(0, NZG // 2, pair_of_steps, 0)
+    for part in range(2):
+        narrow_part(coarse1, eout, sout, NZG - 1, part)
+    store(NZG - 1)
+
+
+def store_copies(eout, sout, ge, gs, sems, t):
+    zr = pl.ds(t * ZG, ZG)
+    return (
+        pltpu.make_async_copy(eout.at[t], ge.at[:, zr], sems.at[t, 0]),
+        pltpu.make_async_copy(sout.at[t], gs.at[zr], sems.at[t, 1]),
+    )
+
+
 def backward_kernel(
-    e_hbm, s_hbm, tab_hbm, coz_hbm, cox_hbm,
+    e_hbm, s_hbm, tab_hbm, coz_hbm, cox_hbm, xst_hbm, ge0_hbm, gs0_hbm,
     ge_hbm, gs_hbm,
     ebuf, sbuf, fine0, fine1, tab, coarse0, coarse1,
     eout, sout, zcar, xcar, coz, cox,
-    in_sem, out_sem, co_sem,
+    in_sem, out_sem, co_sem, pass_sem,
 ):
+    load = Loader(e_hbm, s_hbm, ebuf, sbuf, in_sem, NZG)
     tab_copy = pltpu.make_async_copy(tab_hbm, tab, co_sem.at[0])
-    coz_copy = pltpu.make_async_copy(coz_hbm, coz, co_sem.at[1])
-    cox_copy = pltpu.make_async_copy(cox_hbm, cox.at[pl.ds(0, 4)], co_sem.at[2])
+    handed = (
+        pltpu.make_async_copy(coz_hbm, coz, co_sem.at[1]),
+        pltpu.make_async_copy(cox_hbm, cox, co_sem.at[2]),
+        pltpu.make_async_copy(xst_hbm, xcar, co_sem.at[3]),
+    )
+    passed = [
+        pltpu.make_async_copy(ge0_hbm.at[c], ge_hbm.at[c, :, :, pl.ds(0, HALF), :], pass_sem.at[c]) for c in range(3)
+    ] + [pltpu.make_async_copy(gs0_hbm, gs_hbm.at[:, :, pl.ds(0, HALF), :], pass_sem.at[3])]
     tab_copy.start()
-    load = Loader(e_hbm, s_hbm, ebuf, sbuf, in_sem)
-    for c in load.copies(0):
+    load.start(0, 1)
+    for c in handed:
         c.start()
-    coz_copy.start()
-    cox_copy.start()
-
-    def rest(t, _):
-        for c in load.copies(t):
-            c.start()
-        return 0
-
-    lax.fori_loop(1, STEPS, rest, 0)
+    load.start(1, NZG)
+    for c in passed:
+        c.start()
 
     def stores(t):
-        k, zg = t // NZG, t % NZG
-        zr, xr = pl.ds(zg * ZG, ZG), pl.ds(pl.multiple_of(k * HALF, HALF), HALF)
-        return (
-            pltpu.make_async_copy(eout.at[t], ge_hbm.at[:, zr, :, xr, :], out_sem.at[t, 0]),
-            pltpu.make_async_copy(sout.at[t], gs_hbm.at[zr, :, xr, :], out_sem.at[t, 1]),
-        )
+        xr = pl.ds(HALF, HALF)
+        return store_copies(eout, sout, ge_hbm.at[:, :, :, xr, :], gs_hbm.at[:, :, xr, :], out_sem, t)
 
     def store(t):
         for c in stores(t):
             c.start()
 
+    def ahead_wait(t):
+        @pl.when(t < NZG)
+        def _():
+            load.wait(t)
+
     zcar[0] = jnp.ones_like(zcar[0])
-    xcar[0] = jnp.ones_like(xcar[0])
-    third = jnp.where(lax.broadcasted_iota(jnp.int32, (NSEG, LANE), 1) == 0, 0.0, 1.0 / 3.0)
     tab_copy.wait()
     load.wait(0)
     for part in range(2):
         upsample_part(ebuf, sbuf, 0, tab, fine0, part)
-    coz_copy.wait()
-    cox_copy.wait()
+    for c in handed:
+        c.wait()
     zcar[1] = coz[:, 3]
-    xcar[1] = cox[3]
-    for c in range(3):
-        cox[4 + c] = 0.25 * cox[c]
-
-    def pair_of_steps(i, _):
-        t = i * 2
-        load.wait(t + 1)
-
-        @pl.when(t + 2 < STEPS)
-        def _():
-            load.wait(t + 2)
-
-        for b, (fine, ahead, new, old) in enumerate(((fine0, fine1, coarse0, coarse1), (fine1, fine0, coarse1, coarse0))):
-            before = lax.rem(t + b + STEPS, STEPS + 1)
-            for part in range(2):
-                upsample_part(ebuf, sbuf, t + b + 1, tab, ahead, part)
-                narrow_part(old, eout, sout, before, part)
-                backward_scan(fine, zcar, xcar, coz, cox, new, t // NZG, t % NZG + b, part, third)
-
-        @pl.when(i > 0)
-        def _():
-            store(t - 1)
-
-        store(t)
-        return 0
-
-    lax.fori_loop(0, STEPS // 2, pair_of_steps, 0)
-    for part in range(2):
-        narrow_part(coarse1, eout, sout, STEPS - 1, part)
-    store(STEPS - 1)
+    backward_steps(
+        ahead_wait, lambda i: None, store, ebuf, sbuf, tab, (fine0, fine1), (coarse0, coarse1),
+        eout, sout, zcar, xcar, coz, cox,
+    )
 
     def finish(t, _):
         for c in stores(t):
             c.wait()
         return 0
 
-    lax.fori_loop(0, STEPS, finish, 0)
+    lax.fori_loop(0, NZG, finish, 0)
+    for c in passed:
+        c.wait()
 
 
 def vmem(*shape, dtype=F32):
@@ -632,22 +682,33 @@
     e5 = emission.reshape(3, depth_z, NSEG, SEG, width_y)
     s4 = absorption.reshape(depth_z, NSEG, SEG, width_y)
 
-    buffers = [
-        vmem(STEPS + 1, 3, ZG, NSEG, HALF, LANE, dtype=BF16), vmem(STEPS + 1, ZG, NSEG, HALF, LANE, dtype=BF16),
-        vmem(4, ZG, 2, NSEG * PITCH, LANE), vmem(4, ZG, 2, NSEG * PITCH, LANE),
+    def buffers(steps):
+        return [
+            vmem(steps + 1, 3, ZG, NSEG, HALF, LANE, dtype=BF16), vmem(steps + 1, ZG, NSEG, HALF, LANE, dtype=BF16),
+            vmem(4, ZG, 2, NSEG * PITCH, LANE), vmem(4, ZG, 2, NSEG * PITCH, LANE),
+        ]
+
+    back_buffers = [
+        vmem(3 * LANE, 256, dtype=BF16), vmem(4, ZG, NSEG * PITCH, LANE), vmem(4, ZG, NSEG * PITCH, LANE),
+        vmem(NZG + 1, 3, ZG, NSEG, HALF, LANE, dtype=BF16), vmem(NZG + 1, ZG, NSEG, HALF, LANE, dtype=BF16),
+        vmem(2, HALF, NSEG, 256), vmem(2, 2, NZ * NSEG, LANE),
     ]
     dma = pltpu.SemaphoreType.DMA
-    coz, cox, owned = pl.pallas_call(
+    coz, cox, xst, ge0, gs0, owned = pl.pallas_call(
         functools.partial(forward_kernel, step_z, step_x, 1.0 / (3.0 * pixels * slots)),
         out_shape=[
-            jax.ShapeDtypeStruct((SEG, 4, NSEG, 256), F32),
-            jax.ShapeDtypeStruct((4, 2, NZ * NSEG, LANE), F32),
+            jax.ShapeDtypeStruct((HALF, 4, NSEG, 256), F32),
+            jax.ShapeDtypeStruct((7, 2, NZ * NSEG, LANE), F32),
+            jax.ShapeDtypeStruct((2, 2, NZ * NSEG, LANE), F32),
+            jax.ShapeDtypeStruct((3, NZ, NSEG, HALF, LANE), BF16),
+            jax.ShapeDtypeStruct((NZ, NSEG, HALF, LANE), BF16),
             jax.ShapeDtypeStruct((1, 1), F32),
         ],
-        in_specs=[HBM] * 8,
-        out_specs=[HBM, HBM, pl.BlockSpec(memory_space=pltpu.SMEM)],
-        scratch_shapes=buffers + [
-            vmem(SEG, 4, NSEG, 256), vmem(4, 2, NZ * NSEG, LANE), vmem(SEG, 4, NSEG, 256), vmem(4, 2, NZ * NSEG, LANE),
+        in_specs=[HBM] * 9,
+        out_specs=[HBM] * 5 + [pl.BlockSpec(memory_space=pltpu.SMEM)],
+        scratch_shapes=buffers(STEPS) + [
+            vmem(SEG, 4, NSEG, 256), vmem(4, 2, NZ * NSEG, LANE), vmem(2, HALF, 4, NSEG, 256), vmem(7, 2, NZ * NSEG, LANE),
+        ] + back_buffers + [
             vmem(3, 256, 256, dtype=BF16), vmem(3, NZ, 256, dtype=BF16),
             vmem(3, 2, NSEG * (SEG + 4), LANE), vmem(3, NZ, 256),
             vmem(2, 8, 4, 8, 256), vmem(2, 8, 4, 8, 256), vmem(2, 4, 2, 4, 8, 256), vmem(2, 4, 2, 4, 8, 256),
@@ -656,31 +717,29 @@
             vmem(3 * LANE, 256, dtype=BF16), vmem(256, 256, dtype=BF16), vmem(5, 8, LANE),
             pltpu.SMEM((1, 256), jnp.int32), pltpu.SMEM((1, NZ), jnp.int32),
             vmem(8, 8, LANE), vmem(4, 8, LANE), vmem(4, 8, LANE),
-            dma((STEPS, 2)), dma((6,)), dma((2, 2)), dma((2, 3, 2)), dma((2, 3, 2)), dma((2, 2)), dma((3, 2)), dma((3, 2)),
-            dma((7, 2)), dma((3, 2)), dma((3, 2)), dma((5,)),
+            dma((STEPS, 2)), dma((7,)), dma((2, 2)), dma((2, 3, 2)), dma((2, 3, 2)), dma((2, 2)), dma((3, 2)), dma((3, 2)),
+            dma((7, 2)), dma((3, 2)), dma((3, 2)), dma((3,)), dma((NZG, 2)), dma((NZG // 2,)),
         ],
         compiler_params=pltpu.CompilerParams(
             collective_id=0, has_side_effects=True, vmem_limit_bytes=VMEM_LIMIT
         ),
     )(
         e5, s4, target_z, target_x, owner_z.reshape(count_x, count_y, 1, width_x),
-        owner_x.reshape(count_y, count_z, 1, depth_z), tab, perm,
+        owner_x.reshape(count_y, count_z, 1, depth_z), tab, perm, tab_back,
     )
 
     grad_e, grad_s = pl.pallas_call(
         backward_kernel,
         out_shape=[jax.ShapeDtypeStruct(e5.shape, BF16), jax.ShapeDtypeStruct(s4.shape, BF16)],
-        in_specs=[HBM] * 5,
+        in_specs=[HBM] * 8,
         out_specs=[HBM, HBM],
-        scratch_shapes=buffers + [
-            vmem(3 * LANE, 256, dtype=BF16), vmem(4, ZG, NSEG * PITCH, LANE), vmem(4, ZG, NSEG * PITCH, LANE),
-            vmem(STEPS + 1, 3, ZG, NSEG, HALF, LANE, dtype=BF16), vmem(STEPS + 1, ZG, NSEG, HALF, LANE, dtype=BF16),
-            vmem(2, SEG, NSEG, 256), vmem(2, 2, NZ * NSEG, LANE), vmem(SEG, 4, NSEG, 256), vmem(7, 2, NZ * NSEG, LANE),
-            dma((STEPS, 2)), dma((STEPS, 2)), dma((3,)),
+        scratch_shapes=buffers(NZG) + back_buffers + [
+            vmem(HALF, 4, NSEG, 256), vmem(7, 2, NZ * NSEG, LANE),
+            dma((NZG, 2)), dma((NZG, 2)), dma((4,)), dma((4,)),
         ],
         compiler_params=pltpu.CompilerParams(vmem_limit_bytes=VMEM_LIMIT),
         cost_estimate=pl.CostEstimate(flops=6 * 10**9, bytes_accessed=20 * 2**20, transcendentals=0),
-    )(e5, s4, tab_back, coz, cox)
+    )(e5, s4, tab_back, coz, cox, xst, ge0, gs0)
     return (grad_e.reshape(emission.shape), grad_s.reshape(absorption.shape), owned.reshape(1, 1, 1))
 
 

time: 61.2 us -> 169 us (2.76)
  Pallas kernels: 58.7 us -> 167 us
    pallas_call x1, Pallas kernels: 20.6 us -> 129 us  [local(): pl.pallas_call(backward_kernel, out_shape=[jax.ShapeDtypeStruct(e5.shape,...]
where the time goes in v4:
time: 169 us
  Pallas kernels  167 us (99%)
  between operations  2.34 us (1%)
    pallas_call x1, Pallas kernels, local(): pl.pallas_call(backward_kernel, out_shape=[jax.ShapeDtypeStruct(e5.shape,...  129 us
    pallas_call x1, Pallas kernels, local(): pl.pallas_call(functools.partial(forward_kernel, step_z, step_x, 1.0 / (3...  38.2 us

profile of v4, /device:TPU:1, one launch (start us, length us, event | category | flops | bytes accessed | tf_op | source)
XLA Modules:
  0.0 169.2 jit_solution(4876281194194223749)
XLA Ops:
  0.6 38.2 %shard_map.112 = (f32[16,4,8,256]{3,2,1,0:T(8,128)}, f32[7,2,256,128]{3,2,1,0:T(8,128)}, f32[2,2,256,128]{3,2,1,0:T(8,128)}, bf16[3,32,8,16,128]{4,3,2,1,0:T(8,1...) custom-call(bf16[3,32,8,32,128]{4,3,2,1,0:T(8,128)(2,1)} %bitcast.7, bf16[32,8,32,128]{3,2,1,0:T(8,128)(2,1)} %bitcast.9, ...), custom_call_target="tpu_custom_call" | custom-call | tf_op jit(solution)/shard_map/pallas_call | solution.py:697
  38.8 128.7 %shard_map.113 = (bf16[3,32,8,32,128]{4,3,2,1,0:T(8,128)(2,1)}, bf16[32,8,32,128]{3,2,1,0:T(8,128)(2,1)}) custom-call(bf16[3,32,8,32,128]{4,3,2,1,0:T(8,128)(2,1)} %bitcast.8, bf16[32,8,32,128]{3,2,1,0:T(8,128)(2,1)} %bitcast.10, bf16[384,256]{1,0:T(8,128)(2,1)} %constant.8.clone.back_hbm.tab_hbm, f32[16,4,8,256]{3,2,1,0:T(8,128)} %get-tuple-element.11.coz_hbm, ...), custom_call_target="tpu_custom_call" | custom-call | flops 6000000000 | bytes 20971520 | tf_op jit(solution)/shard_map/pallas_call | solution.py:731

commit v5 on v4

--- a/solution.py
+++ b/solution.py
@@ -598,8 +598,8 @@
     e_hbm, s_hbm, tab_hbm, coz_hbm, cox_hbm, xst_hbm, ge0_hbm, gs0_hbm,
     ge_hbm, gs_hbm,
     ebuf, sbuf, fine0, fine1, tab, coarse0, coarse1,
-    eout, sout, zcar, xcar, coz, cox,
-    in_sem, out_sem, co_sem, pass_sem,
+    eout, sout, zcar, xcar, coz, cox, epass, spass,
+    in_sem, out_sem, co_sem, pass_sem, on_sem,
 ):
     load = Loader(e_hbm, s_hbm, ebuf, sbuf, in_sem, NZG)
     tab_copy = pltpu.make_async_copy(tab_hbm, tab, co_sem.at[0])
@@ -608,16 +608,30 @@
         pltpu.make_async_copy(cox_hbm, cox, co_sem.at[2]),
         pltpu.make_async_copy(xst_hbm, xcar, co_sem.at[3]),
     )
-    passed = [
-        pltpu.make_async_copy(ge0_hbm.at[c], ge_hbm.at[c, :, :, pl.ds(0, HALF), :], pass_sem.at[c]) for c in range(3)
-    ] + [pltpu.make_async_copy(gs0_hbm, gs_hbm.at[:, :, pl.ds(0, HALF), :], pass_sem.at[3])]
+
+    def fetches(t):
+        zr = pl.ds(t * ZG, ZG)
+        return (
+            pltpu.make_async_copy(ge0_hbm.at[:, zr], epass.at[t], pass_sem.at[t, 0]),
+            pltpu.make_async_copy(gs0_hbm.at[zr], spass.at[t], pass_sem.at[t, 1]),
+        )
+
+    def passes(t):
+        xr = pl.ds(0, HALF)
+        return store_copies(epass, spass, ge_hbm.at[:, :, :, xr, :], gs_hbm.at[:, :, xr, :], on_sem, t)
+
     tab_copy.start()
     load.start(0, 1)
     for c in handed:
         c.start()
     load.start(1, NZG)
-    for c in passed:
-        c.start()
+
+    def fetch(t, _):
+        for c in fetches(t):
+            c.start()
+        return 0
+
+    lax.fori_loop(0, NZG, fetch, 0)
 
     def stores(t):
         xr = pl.ds(HALF, HALF)
@@ -625,6 +639,10 @@
 
     def store(t):
         for c in stores(t):
+            c.start()
+        for c in fetches(t):
+            c.wait()
+        for c in passes(t):
             c.start()
 
     def ahead_wait(t):
@@ -646,13 +664,11 @@
     )
 
     def finish(t, _):
-        for c in stores(t):
+        for c in stores(t) + passes(t):
             c.wait()
         return 0
 
     lax.fori_loop(0, NZG, finish, 0)
-    for c in passed:
-        c.wait()
 
 
 def vmem(*shape, dtype=F32):
@@ -735,7 +751,8 @@
         out_specs=[HBM, HBM],
         scratch_shapes=buffers(NZG) + back_buffers + [
             vmem(HALF, 4, NSEG, 256), vmem(7, 2, NZ * NSEG, LANE),
-            dma((NZG, 2)), dma((NZG, 2)), dma((4,)), dma((4,)),
+            vmem(NZG, 3, ZG, NSEG, HALF, LANE, dtype=BF16), vmem(NZG, ZG, NSEG, HALF, LANE, dtype=BF16),
+            dma((NZG, 2)), dma((NZG, 2)), dma((4,)), dma((NZG, 2)), dma((NZG, 2)),
         ],
         compiler_params=pltpu.CompilerParams(vmem_limit_bytes=VMEM_LIMIT),
         cost_estimate=pl.CostEstimate(flops=6 * 10**9, bytes_accessed=20 * 2**20, transcendentals=0),

time: 169 us -> 53.5 us (0.32)
  Pallas kernels: 167 us -> 51.1 us
    pallas_call x1, Pallas kernels: 129 us -> 12.9 us  [local(): pl.pallas_call(backward_kernel, out_shape=[jax.ShapeDtypeStruct(e5.shape,...]
where the time goes in v5:
time: 53.5 us; the launch traced here: 53.4 us
  Pallas kernels  51.1 us (96%)
  between operations  2.34 us (4%)
    pallas_call x1, Pallas kernels, local(): pl.pallas_call(functools.partial(forward_kernel, step_z, step_x, 1.0 / (3...  38.2 us
    pallas_call x1, Pallas kernels, local(): pl.pallas_call(backward_kernel, out_shape=[jax.ShapeDtypeStruct(e5.shape,...  12.9 us

profile of v5, /device:TPU:1, one launch (start us, length us, event | category | flops | bytes accessed | tf_op | source)
XLA Modules:
  0.0 53.4 jit_solution(11049404494979562688)
XLA Ops:
  0.6 38.2 %shard_map.112 = (f32[16,4,8,256]{3,2,1,0:T(8,128)}, f32[7,2,256,128]{3,2,1,0:T(8,128)}, f32[2,2,256,128]{3,2,1,0:T(8,128)}, bf16[3,32,8,16,128]{4,3,2,1,0:T(8,1...) custom-call(bf16[3,32,8,32,128]{4,3,2,1,0:T(8,128)(2,1)} %bitcast.7, bf16[32,8,32,128]{3,2,1,0:T(8,128)(2,1)} %bitcast.9, ...), custom_call_target="tpu_custom_call" | custom-call | tf_op jit(solution)/shard_map/pallas_call | solution.py:713
  38.8 12.9 %shard_map.113 = (bf16[3,32,8,32,128]{4,3,2,1,0:T(8,128)(2,1)}, bf16[32,8,32,128]{3,2,1,0:T(8,128)(2,1)}) custom-call(bf16[3,32,8,32,128]{4,3,2,1,0:T(8,128)(2,1)} %bitcast.8, bf16[32,8,32,128]{3,2,1,0:T(8,128)(2,1)} %bitcast.10, bf16[384,256]{1,0:T(8,128)(2,1)} %constant.8.clone.back_hbm.tab_hbm, f32[16,4,8,256]{3,2,1,0:T(8,128)} %get-tuple-element.11.coz_hbm, ...), custom_call_target="tpu_custom_call" | custom-call | flops 6000000000 | bytes 20971520 | tf_op jit(solution)/shard_map/pallas_call | solution.py:747

commit v6 on v5

--- a/solution.py
+++ b/solution.py
@@ -156,6 +156,8 @@
     ix, iy, iz = lax.axis_index("gx"), lax.axis_index("gy"), lax.axis_index("gz")
     chip, core = iz // 2, iz % 2
     load = Loader(e_hbm, s_hbm, ebuf, sbuf, in_sem, 0)
+    tab_copy = pltpu.make_async_copy(tab_hbm, tab, t_sem.at[4])
+    tab_copy.start()
     load.start(0, STEPS)
     lane = lax.broadcasted_iota(jnp.int32, (8, LANE), 1)
     sub = lax.broadcasted_iota(jnp.int32, (8, LANE), 0)
@@ -165,10 +167,8 @@
     tx_copy = pltpu.make_async_copy(tx_hbm.at[:, pl.ds(pl.multiple_of(iz * NZ, NZ), NZ), px], txb, t_sem.at[1])
     oz_copy = pltpu.make_async_copy(oz_hbm.at[ix, iy], ozb, t_sem.at[2])
     ox_copy = pltpu.make_async_copy(ox_hbm.at[iy, iz], oxb, t_sem.at[3])
-    tab_copy = pltpu.make_async_copy(tab_hbm, tab, t_sem.at[4])
     perm_copy = pltpu.make_async_copy(perm_hbm, perm, t_sem.at[5])
     back_copy = pltpu.make_async_copy(back_hbm, tab_back, t_sem.at[6])
-    tab_copy.start()
     late = (tz_copy, tx_copy, oz_copy, ox_copy, perm_copy, back_copy)
     for c in late:
         c.start()
@@ -599,15 +599,23 @@
     ge_hbm, gs_hbm,
     ebuf, sbuf, fine0, fine1, tab, coarse0, coarse1,
     eout, sout, zcar, xcar, coz, cox, epass, spass,
-    in_sem, out_sem, co_sem, pass_sem, on_sem,
+    in_sem, out_sem, tab_sem, co_sem, hand_sem, pass_sem, on_sem,
 ):
     load = Loader(e_hbm, s_hbm, ebuf, sbuf, in_sem, NZG)
-    tab_copy = pltpu.make_async_copy(tab_hbm, tab, co_sem.at[0])
-    handed = (
-        pltpu.make_async_copy(coz_hbm, coz, co_sem.at[1]),
-        pltpu.make_async_copy(cox_hbm, cox, co_sem.at[2]),
-        pltpu.make_async_copy(xst_hbm, xcar, co_sem.at[3]),
-    )
+    tab_copy = pltpu.make_async_copy(tab_hbm, tab, tab_sem)
+    coz_copy = pltpu.make_async_copy(coz_hbm, coz, co_sem)
+
+    def handed(t):
+        rows = pl.ds(pl.multiple_of(t * ZG * NSEG, ZG * NSEG), ZG * NSEG)
+        return load.copies(t) + (
+            pltpu.make_async_copy(cox_hbm.at[:, :, rows, :], cox.at[:, :, rows, :], hand_sem.at[t, 0]),
+            pltpu.make_async_copy(xst_hbm.at[:, :, rows, :], xcar.at[:, :, rows, :], hand_sem.at[t, 1]),
+        )
+
+    def begin(t, _):
+        for c in handed(t):
+            c.start()
+        return 0
 
     def fetches(t):
         zr = pl.ds(t * ZG, ZG)
@@ -621,10 +629,9 @@
         return store_copies(epass, spass, ge_hbm.at[:, :, :, xr, :], gs_hbm.at[:, :, xr, :], on_sem, t)
 
     tab_copy.start()
-    load.start(0, 1)
-    for c in handed:
-        c.start()
-    load.start(1, NZG)
+    begin(0, 0)
+    coz_copy.start()
+    lax.fori_loop(1, NZG, begin, 0)
 
     def fetch(t, _):
         for c in fetches(t):
@@ -648,15 +655,17 @@
     def ahead_wait(t):
         @pl.when(t < NZG)
         def _():
-            load.wait(t)
+            for c in handed(t):
+                c.wait()
 
     zcar[0] = jnp.ones_like(zcar[0])
     tab_copy.wait()
     load.wait(0)
     for part in range(2):
         upsample_part(ebuf, sbuf, 0, tab, fine0, part)
-    for c in handed:
+    for c in handed(0)[2:]:
         c.wait()
+    coz_copy.wait()
     zcar[1] = coz[:, 3]
     backward_steps(
         ahead_wait, lambda i: None, store, ebuf, sbuf, tab, (fine0, fine1), (coarse0, coarse1),
@@ -752,7 +761,7 @@
         scratch_shapes=buffers(NZG) + back_buffers + [
             vmem(HALF, 4, NSEG, 256), vmem(7, 2, NZ * NSEG, LANE),
             vmem(NZG, 3, ZG, NSEG, HALF, LANE, dtype=BF16), vmem(NZG, ZG, NSEG, HALF, LANE, dtype=BF16),
-            dma((NZG, 2)), dma((NZG, 2)), dma((4,)), dma((NZG, 2)), dma((NZG, 2)),
+            dma((NZG, 2)), dma((NZG, 2)), dma(()), dma(()), dma((NZG, 2)), dma((NZG, 2)), dma((NZG, 2)),
         ],
         compiler_params=pltpu.CompilerParams(vmem_limit_bytes=VMEM_LIMIT),
         cost_estimate=pl.CostEstimate(flops=6 * 10**9, bytes_accessed=20 * 2**20, transcendentals=0),

time: 53.5 us -> 50.6 us (0.946)
  Pallas kernels: 51.1 us -> 48.1 us
    pallas_call x1, Pallas kernels: 38.2 us -> 35.7 us  [local(): pl.pallas_call(functools.partial(forward_kernel, step_z, step_x, 1.0 / (3...]
where the time goes in v6:
time: 50.6 us; the launch traced here: 50.5 us
  Pallas kernels  48.1 us (95%)
  between operations  2.34 us (5%)
    pallas_call x1, Pallas kernels, local(): pl.pallas_call(functools.partial(forward_kernel, step_z, step_x, 1.0 / (3...  35.7 us
    pallas_call x1, Pallas kernels, local(): pl.pallas_call(backward_kernel, out_shape=[jax.ShapeDtypeStruct(e5.shape,...  12.4 us

profile of v6, /device:TPU:1, one launch (start us, length us, event | category | flops | bytes accessed | tf_op | source)
XLA Modules:
  0.0 50.5 jit_solution(5321931616815853178)
XLA Ops:
  0.6 35.7 %shard_map.112 = (f32[16,4,8,256]{3,2,1,0:T(8,128)}, f32[7,2,256,128]{3,2,1,0:T(8,128)}, f32[2,2,256,128]{3,2,1,0:T(8,128)}, bf16[3,32,8,16,128]{4,3,2,1,0:T(8,1...) custom-call(bf16[3,32,8,32,128]{4,3,2,1,0:T(8,128)(2,1)} %bitcast.7, bf16[32,8,32,128]{3,2,1,0:T(8,128)(2,1)} %bitcast.9, ...), custom_call_target="tpu_custom_call" | custom-call | tf_op jit(solution)/shard_map/pallas_call | solution.py:722
  36.3 12.4 %shard_map.113 = (bf16[3,32,8,32,128]{4,3,2,1,0:T(8,128)(2,1)}, bf16[32,8,32,128]{3,2,1,0:T(8,128)(2,1)}) custom-call(bf16[3,32,8,32,128]{4,3,2,1,0:T(8,128)(2,1)} %bitcast.8, bf16[32,8,32,128]{3,2,1,0:T(8,128)(2,1)} %bitcast.10, bf16[384,256]{1,0:T(8,128)(2,1)} %constant.8.clone.back_hbm.tab_hbm, f32[16,4,8,256]{3,2,1,0:T(8,128)} %get-tuple-element.11.coz_hbm, ...), custom_call_target="tpu_custom_call" | custom-call | flops 6000000000 | bytes 20971520 | tf_op jit(solution)/shard_map/pallas_call | solution.py:756

commit v7 on v6

--- a/solution.py
+++ b/solution.py
@@ -228,7 +228,12 @@
                     pc[k, m, i, :, half(h)] = v
             return 0
 
-        lax.fori_loop(0, 8, body, 0)
+        def four(n, _):
+            for u in range(4):
+                body(n * 4 + u, 0)
+            return 0
+
+        lax.fori_loop(0, 2, four, 0)
         for c in chip_copies(k):
             c.start()
 
@@ -273,7 +278,12 @@
                     fin[k, m, f, :, hs] = jnp.where(first, part_b[f], part_a[f])
             return 0
 
-        lax.fori_loop(0, 8, body, 0)
+        def four(n, _):
+            for u in range(4):
+                body(n * 4 + u, 0)
+            return 0
+
+        lax.fori_loop(0, 2, four, 0)
         fin_copy(k).start()
 
     mine, other = pl.ds(core * 8, 8), pl.ds((1 - core) * 8, 8)
@@ -328,12 +338,11 @@
                 front = jnp.ones((8, LANE), F32)
                 for s in range(NSEG):
                     rows = pl.ds(g * 64 + s, 8, stride=NSEG)
-                    cox[0, h, rows, :] = front * g0
-                    cox[1, h, rows, :] = front * g1
-                    cox[2, h, rows, :] = front * g2
+                    for c, colour in enumerate((g0, g1, g2)):
+                        v = front * colour
+                        cox[c, h, rows, :] = v
+                        cox[4 + c, h, rows, :] = 0.25 * v
                     cox[3, h, rows, :] = front * xsuf[s] * (-step_x)
-                    for c in range(3):
-                        cox[4 + c, h, rows, :] = 0.25 * cox[c, h, rows, :]
                     front = front * xc[3, h, rows, :]
         cox_copy.start()
 

time: 50.6 us -> 50.5 us (level)
  no operation moved by 1% of the time
where the time goes in v7:
time: 50.5 us; the launch traced here: 50.4 us
  Pallas kernels  48.1 us (95%)
  between operations  2.34 us (5%)
    pallas_call x1, Pallas kernels, local(): pl.pallas_call(functools.partial(forward_kernel, step_z, step_x, 1.0 / (3...  35.6 us
    pallas_call x1, Pallas kernels, local(): pl.pallas_call(backward_kernel, out_shape=[jax.ShapeDtypeStruct(e5.shape,...  12.4 us

profile of v7, /device:TPU:1, one launch (start us, length us, event | category | flops | bytes accessed | tf_op | source)
XLA Modules:
  0.0 50.4 jit_solution(113383475068891541)
XLA Ops:
  0.6 35.6 %shard_map.112 = (f32[16,4,8,256]{3,2,1,0:T(8,128)}, f32[7,2,256,128]{3,2,1,0:T(8,128)}, f32[2,2,256,128]{3,2,1,0:T(8,128)}, bf16[3,32,8,16,128]{4,3,2,1,0:T(8,1...) custom-call(bf16[3,32,8,32,128]{4,3,2,1,0:T(8,128)(2,1)} %bitcast.7, bf16[32,8,32,128]{3,2,1,0:T(8,128)(2,1)} %bitcast.9, ...), custom_call_target="tpu_custom_call" | custom-call | tf_op jit(solution)/shard_map/pallas_call | solution.py:731
  36.3 12.4 %shard_map.113 = (bf16[3,32,8,32,128]{4,3,2,1,0:T(8,128)(2,1)}, bf16[32,8,32,128]{3,2,1,0:T(8,128)(2,1)}) custom-call(bf16[3,32,8,32,128]{4,3,2,1,0:T(8,128)(2,1)} %bitcast.8, bf16[32,8,32,128]{3,2,1,0:T(8,128)(2,1)} %bitcast.10, bf16[384,256]{1,0:T(8,128)(2,1)} %constant.8.clone.back_hbm.tab_hbm, f32[16,4,8,256]{3,2,1,0:T(8,128)} %get-tuple-element.11.coz_hbm, ...), custom_call_target="tpu_custom_call" | custom-call | flops 6000000000 | bytes 20971520 | tf_op jit(solution)/shard_map/pallas_call | solution.py:765
